TPU v7x, 256 devices: a whole 4x4x8 slice. The times are simulated.
256 devices in a mesh: cuts: 16 (over z, core), row: 16 (over y, x).
Axes of the slice: x: 4, y: 4, z: 8, core: 2. Of those that a mesh axis runs over, the one named last changes fastest.
Arguments:
- diagonal_blocks: bfloat16 [32, 2, 1024, 1024], P('cuts', None, 'row'), as said below
- diagonal_inverses: bfloat16 [32, 2, 1024, 1024], P('cuts', None, 'row'), as said below
- lower_blocks: bfloat16 [32, 2, 1024, 1024], P('cuts', None, 'row'), may hold values from -0.140625 to 0.140625
- upper_blocks: bfloat16 [32, 2, 1024, 1024], P('cuts', None, 'row'), may hold values from -0.140625 to 0.140625
- injection: bfloat16 [32, 2, 1024, 128], P('cuts', None, 'row'), may hold values from -6 to 6
- orbitals: int32 [32], replicated, may hold values from 512 to 1024, as said below
Outputs:
- reduced_diagonal: bfloat16 [16, 2, 1024, 1024], P('cuts', None, 'row')
- reduced_lower: bfloat16 [16, 2, 1024, 1024], P('cuts', None, 'row')
- reduced_upper: bfloat16 [16, 2, 1024, 1024], P('cuts', None, 'row')
- reduced_rhs: float32 [16, 2, 1024, 128], P('cuts', None, 'row')
- block_solutions: float32 [16, 2, 1024, 128], P('cuts', None, 'row')
Inputs may be any that keep to these rules, and one draw needn't show every extreme that they name: Active orbitals of each slice, at least half of 1024; block rows and columns at or beyond the count are inactive; some slice has all 1024. `diagonal_blocks`: diagonal blocks, a varying diagonal plus a dense part. `diagonal_inverses`: approximate inverses of the diagonal blocks.
All inputs are finite; a program needn't handle non-finite values.
Results may differ from a plain program's by a relative error of at most 0.014.
Values may be sent and summed in bfloat16 or wider, within the bound.
No kernel may reach another device: no remote copies, remote signals or barrier semaphores. Data moves between devices by JAX's collectives and lax.ppermute only.
A program may use at most 64 MiB of HBM per device.

v0:
```python
import jax
import jax.numpy as jnp
from jax import lax
from jax.sharding import PartitionSpec as P

REFINE = 2


def passed_along(shard, axis, by):
    length = lax.axis_size(axis)
    pairs = [(i, i + by) for i in range(length) if 0 <= i + by < length]
    return lax.ppermute(shard, axis, pairs)


def complex_product(left_block, right_block):
    real_part = jnp.dot(
        left_block[0], right_block[0], preferred_element_type=jnp.float32
    ) - jnp.dot(left_block[1], right_block[1], preferred_element_type=jnp.float32)
    imag_part = jnp.dot(
        left_block[0], right_block[1], preferred_element_type=jnp.float32
    ) + jnp.dot(left_block[1], right_block[0], preferred_element_type=jnp.float32)
    return jnp.stack([real_part, imag_part])


def multiply_rows(left_blocks, pieces):
    results = []
    for left_block in left_blocks:
        for piece in pieces:
            results.append(complex_product(left_block, piece))
    return tuple((result for result in results))


def single_rows(left_block, piece):
    return complex_product(left_block, piece)


def body(diagonal_blocks, diagonal_inverses, lower_blocks, upper_blocks, injection, orbitals):
    device = lax.axis_index("cuts")
    panel_index = lax.axis_index("row")
    panel_rows = diagonal_blocks.shape[2]
    block_order = diagonal_blocks.shape[3]
    empty_count = jnp.zeros((1,), jnp.int32)
    padded = jnp.concatenate([empty_count, orbitals, empty_count])
    window = lax.dynamic_slice_in_dim(padded, 2 * device, 4)
    places_row = panel_index * panel_rows + jnp.arange(panel_rows, dtype=jnp.int32)
    places_col = jnp.arange(block_order, dtype=jnp.int32)

    def slice_masks(local):
        row_on = places_row < window[local + 1]
        lower_on = row_on[:, None] & (places_col[None, :] < window[local])
        upper_on = row_on[:, None] & (places_col[None, :] < window[local + 2])
        return (
            row_on.astype(jnp.bfloat16),
            lower_on.astype(jnp.bfloat16),
            upper_on.astype(jnp.bfloat16),
        )

    row_even, lower_even, upper_even = slice_masks(0)
    row_odd, lower_odd, upper_odd = slice_masks(1)
    lower_first = lower_blocks[0] * lower_even[None]
    upper_first = upper_blocks[0] * upper_even[None]
    source_first = injection[0] * row_even[None, :, None]
    lower_second = lower_blocks[1] * lower_odd[None]
    upper_second = upper_blocks[1] * upper_odd[None]
    source_second = injection[1] * row_odd[None, :, None]
    inverse_odd = diagonal_inverses[1]
    p_own, q_own, y_own = multiply_rows(
        (inverse_odd,),
        (
            lax.all_gather(upper_second, "row", axis=1, tiled=True),
            lax.all_gather(lower_second, "row", axis=1, tiled=True),
            lax.all_gather(source_second, "row", axis=1, tiled=True),
        ),
    )
    p_own = p_own.astype(jnp.bfloat16)
    q_own = q_own.astype(jnp.bfloat16)
    y_own = y_own.astype(jnp.bfloat16)
    upper_p, upper_q, upper_y = multiply_rows(
        (upper_first,),
        (
            lax.all_gather(p_own, "row", axis=1, tiled=True),
            lax.all_gather(q_own, "row", axis=1, tiled=True),
            lax.all_gather(y_own, "row", axis=1, tiled=True),
        ),
    )
    carried_p, carried_q, carried_y = passed_along((p_own, q_own, y_own), "cuts", 1)
    lower_p, lower_q, lower_y = multiply_rows(
        (lower_first,),
        (
            lax.all_gather(carried_p, "row", axis=1, tiled=True),
            lax.all_gather(carried_q, "row", axis=1, tiled=True),
            lax.all_gather(carried_y, "row", axis=1, tiled=True),
        ),
    )
    diagonal_new = (diagonal_blocks[0].astype(jnp.float32) - lower_p - upper_q).astype(jnp.bfloat16)
    lower_new = (-lower_q).astype(jnp.bfloat16)
    upper_new = (-upper_p).astype(jnp.bfloat16)
    source_new = (source_first.astype(jnp.float32) - lower_y - upper_y).astype(jnp.bfloat16)
    inverse_even = diagonal_inverses[0]
    iterate = single_rows(
        inverse_even, lax.all_gather(source_new, "row", axis=1, tiled=True)
    ).astype(jnp.bfloat16)
    for refine_turn in range(REFINE):
        applied = single_rows(diagonal_new, lax.all_gather(iterate, "row", axis=1, tiled=True))
        residue = (source_new.astype(jnp.float32) - applied).astype(jnp.bfloat16)
        correction = single_rows(inverse_even, lax.all_gather(residue, "row", axis=1, tiled=True))
        iterate = (iterate.astype(jnp.float32) + correction).astype(jnp.bfloat16)
    solved_below = passed_along(iterate, "cuts", 1)
    solved_above = passed_along(iterate, "cuts", -1)
    coupled_lower = complex_product(
        lower_new, lax.all_gather(solved_below, "row", axis=1, tiled=True)
    )
    coupled_upper = complex_product(
        upper_new, lax.all_gather(solved_above, "row", axis=1, tiled=True)
    )
    combined = source_new.astype(jnp.float32) - coupled_lower - coupled_upper
    return (
        diagonal_new[None],
        lower_new[None],
        upper_new[None],
        combined[None],
        iterate.astype(jnp.float32)[None],
    )


def solution(mesh):
    return jax.shard_map(
        body,
        mesh=mesh,
        in_specs=(
            P("cuts", None, "row", None),
            P("cuts", None, "row", None),
            P("cuts", None, "row", None),
            P("cuts", None, "row", None),
            P("cuts", None, "row", None),
            P(),
        ),
        out_specs=(
            P("cuts", None, "row", None),
            P("cuts", None, "row", None),
            P("cuts", None, "row", None),
            P("cuts", None, "row", None),
            P("cuts", None, "row", None),
        ),
        check_vma=False,
    )
```

profile of v0, /device:TPU:32, one launch (start us, length us, event | category | flops | bytes accessed | tf_op | source)
XLA Modules:
  0.0 460.9 jit_solution(11540268364108531146)
XLA Ops:
  14.7 1.8 bitcast_multiply_fusion
  16.6 57.5 %all-gather.7.cloned.1.call-done = bf16[2,1024,1024]{2,1,0:T(8,128)(2,1)} async-done(((bf16[2,64,1024]{2,1,0:T(8,128)(2,1)}), bf16[2,1024,1024]{2,1,0:T(8,128)(2,1)}) %all-gather.7.cloned.1.call-update) | async-done | bytes 4194320 | tf_op jit(solution)/shard_map/all_gather | solution.py:70
  74.0 2.3 fusion
  76.3 2.1 fusion.43
  80.2 53.3 %all-gather.11.cloned.1.call-done = bf16[2,1024,1024]{2,1,0:T(8,128)(2,1)} async-done(((bf16[2,64,1024]{2,1,0:T(8,128)(2,1)}), bf16[2,1024,1024]{2,1,0:T(8,128)(2,1)}) %all-gather.11.cloned.1.call-update) | async-done | bytes 4194320 | tf_op jit(solution)/shard_map/all_gather | solution.py:71
  133.5 2.2 fusion.9
  135.7 2.1 fusion.40
  139.7 1.9 collective-permute-start
  141.6 5.8 %collective-permute-done = bf16[2,64,1024]{2,1,0:T(8,128)(2,1)S(1)} collective-permute-done((bf16[2,64,1024]{2,1,0:T(8,128)(2,1)S(1)}, bf16[2,64,1024]{2,1,0:T(8,128)(2,1)S(1)}, u32[]{:S(2)}, u32[]{:S(2)}) %collective-permute-start) | collective-permute-done | bytes 262176 | tf_op jit(solution)/shard_map/ppermute | solution.py:12
  148.2 23.7 %all_gather.54 = bf16[2,1024,128]{2,1,0:T(8,128)(2,1)S(1)} all-gather(bf16[2,64,128]{2,1,0:T(8,128)(2,1)S(1)} %bitcast_multiply_fusion.5), channel_id=1, replica_groups=mesh['cuts'=16,'row'=16] {'row'}, dimensions={1}, use_global_device_ids=true | all-gather | bytes 557056 | tf_op jit(solution)/shard_map/all_gather | solution.py:72
  172.7 1.9 collective-permute-start.2
  174.6 23.0 %all_gather.56 = bf16[2,1024,128]{2,1,0:T(8,128)(2,1)S(1)} all-gather(bf16[2,64,128]{2,1,0:T(8,128)(2,1)S(1)} %pad_maximum_fusion.2), channel_id=1, replica_groups=mesh['cuts'=16,'row'=16] {'row'}, dimensions={1}, use_global_device_ids=true | all-gather | bytes 557056 | tf_op jit(solution)/shard_map/all_gather | solution.py:83
  198.4 23.9 %all_gather.55 = bf16[2,1024,128]{2,1,0:T(8,128)(2,1)S(1)} all-gather(bf16[2,64,128]{2,1,0:T(8,128)(2,1)S(1)} %collective-permute-done.2), channel_id=1, replica_groups=mesh['cuts'=16,'row'=16] {'row'}, dimensions={1}, use_global_device_ids=true | all-gather | bytes 557056 | tf_op jit(solution)/shard_map/all_gather | solution.py:92
  223.1 22.6 %all_gather.57 = bf16[2,1024,128]{2,1,0:T(8,128)(2,1)S(1)} all-gather(bf16[2,64,128]{2,1,0:T(8,128)(2,1)S(1)} %fusion.116), channel_id=1, replica_groups=mesh['cuts'=16,'row'=16] {'row'}, dimensions={1}, use_global_device_ids=true | all-gather | bytes 557056 | tf_op jit(solution)/shard_map/all_gather | solution.py:101
  246.2 1.9 collective-permute-start.1
  248.4 24.0 %all_gather.58 = bf16[2,1024,128]{2,1,0:T(8,128)(2,1)S(1)} all-gather(bf16[2,64,128]{2,1,0:T(8,128)(2,1)S(1)} %pad_maximum_fusion.3), channel_id=1, replica_groups=mesh['cuts'=16,'row'=16] {'row'}, dimensions={1}, use_global_device_ids=true | all-gather | bytes 557056 | tf_op jit(solution)/shard_map/all_gather | solution.py:104
  273.2 2.2 fusion.21
  275.4 2.1 fusion.20
  279.2 2.2 fusion.13
  281.5 2.1 fusion.12
  284.6 31.1 %all-gather.9.cloned.1.call-done = bf16[2,1024,1024]{2,1,0:T(8,128)(2,1)} async-done(((bf16[2,64,1024]{2,1,0:T(8,128)(2,1)}), bf16[2,1024,1024]{2,1,0:T(8,128)(2,1)}) %all-gather.9.cloned.1.call-update) | async-done | bytes 4194320 | tf_op jit(solution)/shard_map/all_gather | solution.py:90
  315.7 2.2 fusion.7
  318.0 2.1 fusion.4
  322.0 24.1 %all_gather.59 = bf16[2,1024,128]{2,1,0:T(8,128)(2,1)S(1)} all-gather(bf16[2,64,128]{2,1,0:T(8,128)(2,1)S(1)} %fusion.111), channel_id=1, replica_groups=mesh['cuts'=16,'row'=16] {'row'}, dimensions={1}, use_global_device_ids=true | all-gather | bytes 557056 | tf_op jit(solution)/shard_map/all_gather | solution.py:106
  346.9 23.3 %all_gather.60 = bf16[2,1024,128]{2,1,0:T(8,128)(2,1)S(1)} all-gather(bf16[2,64,128]{2,1,0:T(8,128)(2,1)S(1)} %fusion.117), channel_id=1, replica_groups=mesh['cuts'=16,'row'=16] {'row'}, dimensions={1}, use_global_device_ids=true | all-gather | bytes 557056 | tf_op jit(solution)/shard_map/all_gather | solution.py:104
  371.1 22.9 %all_gather.61 = bf16[2,1024,128]{2,1,0:T(8,128)(2,1)S(1)} all-gather(bf16[2,64,128]{2,1,0:T(8,128)(2,1)S(1)} %fusion.112), channel_id=1, replica_groups=mesh['cuts'=16,'row'=16] {'row'}, dimensions={1}, use_global_device_ids=true | all-gather | bytes 557056 | tf_op jit(solution)/shard_map/all_gather | solution.py:106
  394.7 1.9 collective-permute-start.4
  396.7 2.4 collective-permute-start.3
  399.1 2.2 fusion.19
  401.4 2.1 fusion.16
  406.6 22.2 %all_gather.63 = bf16[2,1024,128]{2,1,0:T(8,128)(2,1)S(1)} all-gather(bf16[2,64,128]{2,1,0:T(8,128)(2,1)S(1)} %collective-permute-done.4), channel_id=1, replica_groups=mesh['cuts'=16,'row'=16] {'row'}, dimensions={1}, use_global_device_ids=true | all-gather | bytes 557056 | tf_op jit(solution)/shard_map/all_gather | solution.py:114
  429.3 23.0 %all_gather.62 = bf16[2,1024,128]{2,1,0:T(8,128)(2,1)S(1)} all-gather(bf16[2,64,128]{2,1,0:T(8,128)(2,1)S(1)} %collective-permute-done.3), channel_id=1, replica_groups=mesh['cuts'=16,'row'=16] {'row'}, dimensions={1}, use_global_device_ids=true | all-gather | bytes 557056 | tf_op jit(solution)/shard_map/all_gather | solution.py:111
  (129 shorter events, 27.8 us)
Async XLA Ops:
  7.2 69.2 %copy-start.12 = (bf16[2,2,64,1024]{3,2,1,0:T(8,128)(2,1)S(1)}, bf16[2,2,64,1024]{3,2,1,0:T(8,128)(2,1)}, u32[]{:S(2)}) copy-start(bf16[2,2,64,1024]{3,2,1,0:T(8,128)(2,1)} %param.7) | copy-start | bytes 1572868
  7.2 66.9 %all-gather.7.cloned.1.call-start = ((), (), s32[]{:S(2)}) async-start(), calls=%async_computation | async-start | bytes 4456448 | tf_op jit(solution)/shard_map/all_gather | solution.py:70
  14.7 118.8 %all-gather.11.cloned.1.call-start = ((), (), s32[]{:S(2)}) async-start(), calls=%async_computation.2 | async-start | bytes 4456448 | tf_op jit(solution)/shard_map/all_gather | solution.py:71
  16.5 256.6 %all-gather.17.cloned.1.call-start = ((), (), s32[]{:S(2)}) async-start(), calls=%async_computation.5 | async-start | bytes 4456448 | tf_op jit(solution)/shard_map/all_gather | solution.py:81
  74.0 4.4 copy-start.11
  80.2 199.1 %all-gather.13.cloned.1.call-start = ((), (), s32[]{:S(2)}) async-start(), calls=%async_computation.3 | async-start | bytes 4456448 | tf_op jit(solution)/shard_map/all_gather | solution.py:82
  133.5 4.4 copy-start.10
  135.7 3.9 copy-start.4
  135.7 12.4 %copy-start.7 = (bf16[2,2,64,128]{3,2,1,0:T(8,128)(2,1)S(1)}, bf16[2,2,64,128]{3,2,1,0:T(8,128)(2,1)}, u32[]{:S(2)}) copy-start(bf16[2,2,64,128]{3,2,1,0:T(8,128)(2,1)} %param.10) | copy-start | bytes 196612
  139.6 176.1 %all-gather.9.cloned.1.call-start = ((), (), s32[]{:S(2)}) async-start(), calls=%async_computation.1 | async-start | bytes 4456448 | tf_op jit(solution)/shard_map/all_gather | solution.py:90
  139.7 7.7 %collective-permute-start = (bf16[2,64,1024]{2,1,0:T(8,128)(2,1)S(1)}, bf16[2,64,1024]{2,1,0:T(8,128)(2,1)S(1)}, u32[]{:S(2)}, u32[]{:S(2)}) collective-permute-start(bf16[2,64,1024]{2,1,0:T(8,128)(2,1)S(1)} %copy-done.4), channel_id=1, source_target_pairs={{0,16},{16,32},{32,48},{48,64},{64,80},{80,96},{96,112},{112,128},... | collective-permute-start | bytes 786440 | tf_op jit(solution)/shard_map/ppermute | solution.py:12
  147.3 0.7 copy-start.8
  148.1 251.0 %all-gather.15.cloned.1.call-start = ((), (), s32[]{:S(2)}) async-start(), calls=%async_computation.4 | async-start | bytes 4456448 | tf_op jit(solution)/shard_map/all_gather | solution.py:91
  171.9 74.1 %copy-start.13 = (bf16[2,2,64,1024]{3,2,1,0:T(8,128)(2,1)S(1)}, bf16[2,2,64,1024]{3,2,1,0:T(8,128)(2,1)}, u32[]{:S(2)}) copy-start(bf16[2,2,64,1024]{3,2,1,0:T(8,128)(2,1)} %param.7) | copy-start | bytes 1572868
  172.1 74.2 %copy-start.5 = (bf16[2,64,1024]{2,1,0:T(8,128)(2,1)S(1)}, bf16[2,64,1024]{2,1,0:T(8,128)(2,1)}, u32[]{:S(2)}) copy-start(bf16[2,64,1024]{2,1,0:T(8,128)(2,1)} %pad_maximum_fusion.1) | copy-start | bytes 786436
  172.7 25.7 %collective-permute-start.2 = (bf16[2,64,128]{2,1,0:T(8,128)(2,1)S(1)}, bf16[2,64,128]{2,1,0:T(8,128)(2,1)S(1)}, u32[]{:S(2)}, u32[]{:S(2)}) collective-permute-start(bf16[2,64,128]{2,1,0:T(8,128)(2,1)S(1)} %pad_maximum_fusion.2), channel_id=1, source_target_pairs={{0,16},{16,32},{32,48},{48,64},{64,80},{80,96},{96,112},{112,128},... | collective-permute-start | bytes 98312 | tf_op jit(solution)/shard_map/ppermute | solution.py:12
  246.2 26.1 %collective-permute-start.1 = (bf16[2,64,1024]{2,1,0:T(8,128)(2,1)S(1)}, bf16[2,64,1024]{2,1,0:T(8,128)(2,1)S(1)}, u32[]{:S(2)}, u32[]{:S(2)}) collective-permute-start(bf16[2,64,1024]{2,1,0:T(8,128)(2,1)S(1)} %copy-done.5), channel_id=1, source_target_pairs={{0,16},{16,32},{32,48},{48,64},{64,80},{80,96},{96,112},{112,128},... | collective-permute-start | bytes 786440 | tf_op jit(solution)/shard_map/ppermute | solution.py:12
  272.4 0.7 copy-start.9
  273.2 4.3 copy-start
  279.2 4.4 copy-start.1
  315.7 4.4 copy-start.2
  318.0 3.1 copy-start.6
  320.1 26.0 %copy-start.14 = (bf16[2,2,64,1024]{3,2,1,0:T(8,128)(2,1)S(1)}, bf16[2,2,64,1024]{3,2,1,0:T(8,128)(2,1)}, u32[]{:S(2)}) copy-start(bf16[2,2,64,1024]{3,2,1,0:T(8,128)(2,1)} %param.7) | copy-start | bytes 1572868
  394.7 11.9 %collective-permute-start.4 = (bf16[2,64,128]{2,1,0:T(8,128)(2,1)S(1)}, bf16[2,64,128]{2,1,0:T(8,128)(2,1)S(1)}, u32[]{:S(2)}, u32[]{:S(2)}) collective-permute-start(bf16[2,64,128]{2,1,0:T(8,128)(2,1)S(1)} %fusion.118), channel_id=1, source_target_pairs={{16,0},{32,16},{48,32},{64,48},{80,64},{96,80},{112,96},{128,112},... | collective-permute-start | bytes 98312 | tf_op jit(solution)/shard_map/ppermute | solution.py:12
  396.7 32.6 %collective-permute-start.3 = (bf16[2,64,128]{2,1,0:T(8,128)(2,1)S(1)}, bf16[2,64,128]{2,1,0:T(8,128)(2,1)S(1)}, u32[]{:S(2)}, u32[]{:S(2)}) collective-permute-start(bf16[2,64,128]{2,1,0:T(8,128)(2,1)S(1)} %fusion.118), channel_id=1, source_target_pairs={{0,16},{16,32},{32,48},{48,64},{64,80},{80,96},{96,112},{112,128},... | collective-permute-start | bytes 98312 | tf_op jit(solution)/shard_map/ppermute | solution.py:12
  399.1 4.3 copy-start.3
Sparse Core Ops, SparseCore 0:
  14.8 59.2 all-gather.6
  77.0 56.3 all-gather.10
  136.5 58.6 all-gather.16
  198.1 58.3 all-gather.12
  259.3 56.4 all-gather.8
  318.0 58.8 all-gather.14
where the time goes:
time: 462 us; the launch traced here: 461 us
  blocking collectives  233 us (50%)
  waiting for transfers between devices  148 us (32%)
  matrix products  38.9 us (8%)
  between operations  14.9 us (3%)
  other arithmetic  14.1 us (3%)
  starting transfers between devices  10.3 us (2%)
    all_gather x1, waiting for transfers between devices, body(): lax.all_gather(upper_second, 'row', axis=1, tiled=True)  57.5 us
    all_gather x1, waiting for transfers between devices, body(): lax.all_gather(lower_second, 'row', axis=1, tiled=True)  53.3 us
    all_gather x2, blocking collectives, body(): lax.all_gather(iterate, 'row', axis=1, tiled=True)  47.3 us
    all_gather x2, blocking collectives, body(): lax.all_gather(residue, 'row', axis=1, tiled=True)  47 us
    all_gather x1, waiting for transfers between devices, body(): lax.all_gather(carried_p, 'row', axis=1, tiled=True)  31.1 us
    all_gather x1, blocking collectives, body(): lax.all_gather(carried_y, 'row', axis=1, tiled=True)  23.9 us
    all_gather x1, blocking collectives, body(): lax.all_gather(source_second, 'row', axis=1, tiled=True)  23.7 us
    all_gather x1, blocking collectives, body(): lax.all_gather(y_own, 'row', axis=1, tiled=True)  23 us
  transfers between devices with their start and end apart: 11, of which 4 were waited for; matrix products, arithmetic and copies ran while one was open for 10% of the time, Pallas kernels for 0%

commit v1 on v0

v1 whole, which is shorter than its diff:
```python
import functools

import jax
import jax.numpy as jnp
from jax import lax
from jax.experimental import pallas as pl
from jax.experimental.pallas import tpu as pltpu
from jax.sharding import PartitionSpec as P

REFINE = 2
BF = jnp.bfloat16
F32 = jnp.float32
VMEM = pl.BlockSpec(memory_space=pltpu.VMEM)
SMEM = pl.BlockSpec(memory_space=pltpu.SMEM)


def call(kernel, out_shapes, flops, *args):
    moved = sum(a.size * a.dtype.itemsize for a in args) + sum(
        s.size * s.dtype.itemsize for s in out_shapes
    )
    return pl.pallas_call(
        kernel,
        out_shape=tuple(out_shapes),
        in_specs=[SMEM] + [VMEM] * (len(args) - 1),
        out_specs=tuple([VMEM] * len(out_shapes)),
        compiler_params=pltpu.CompilerParams(vmem_limit_bytes=40 * 1024 * 1024),
        cost_estimate=pl.CostEstimate(flops=flops, bytes_accessed=moved, transcendentals=0),
    )(*args)


def shape(dims, dtype=BF):
    return jax.ShapeDtypeStruct(dims, dtype)


def mod4(v):
    return lax.rem(v + 8, 4)


def lanes_of(rows):
    return lax.broadcasted_iota(jnp.int32, (rows, 128), 1)


def combine_small(real_rows, imag_rows):
    lane = lanes_of(real_rows.shape[0])
    turned = jnp.where(lane < 32, -pltpu.roll(imag_rows, 96, 1), pltpu.roll(imag_rows, 32, 1))
    return jnp.where(lane < 64, real_rows + turned, 0.0)


def prepare_kernel(s_ref, d_ref, g_ref, a_ref, c_ref, b_ref,
                   piece0, piece1, piece2, piece3, g_odd, g_even, a_even, c_even):
    y, x = s_ref[0], s_ref[1]
    first_row = (y * 4 + x) * 64
    before, own, odd, after = s_ref[2], s_ref[3], s_ref[4], s_ref[5]
    row = first_row + lax.broadcasted_iota(jnp.int32, (64, 256), 0)
    col = lax.broadcasted_iota(jnp.int32, (64, 256), 1)
    row_b = first_row + lax.broadcasted_iota(jnp.int32, (64, 128), 0)
    lane = lanes_of(64)

    def masked(block, rows_on, chunk, cols_on):
        on = (row < rows_on) & (col + chunk * 256 < cols_on)
        return jnp.where(on, block.astype(F32), 0.0).astype(BF)

    for shift, piece in enumerate((piece0, piece1, piece2, piece3)):
        chunk = mod4(x + shift)
        cols = pl.ds(pl.multiple_of(chunk * 256, 256), 256)
        for part in range(2):
            piece[:, pl.ds(part * 256, 256)] = masked(c_ref[1, part, :, cols], odd, chunk, after)
            piece[:, pl.ds(512 + part * 256, 256)] = masked(a_ref[1, part, :, cols], odd, chunk, own)
            piece[:, pl.ds(1152 + part * 256, 256)] = d_ref[0, part, :, cols]
        tile = jnp.zeros((64, 128), F32)
        for place, (which, part, rows_on) in enumerate(
            ((1, 0, odd), (1, 1, odd), (0, 0, own), (0, 1, own))
        ):
            block = jnp.where(row_b < rows_on, b_ref[which, part].astype(F32), 0.0)
            turned = pltpu.roll(block, mod4(place - chunk) * 32, 1)
            tile = jnp.where((lane >= place * 32) & (lane < place * 32 + 32), turned, tile)
        piece[:, pl.ds(1024, 128)] = tile.astype(BF)
    for place in range(4):
        chunk = mod4(y + place)
        cols = pl.ds(pl.multiple_of(chunk * 256, 256), 256)
        out = pl.ds(place * 256, 256)
        for part in range(2):
            g_odd[part, :, out] = g_ref[1, part, :, cols]
            g_even[part, :, out] = g_ref[0, part, :, cols]
            a_even[part, :, out] = masked(a_ref[0, part, :, cols], own, chunk, before)
            c_even[part, :, out] = masked(c_ref[0, part, :, cols], own, chunk, odd)


def assemble_kernel(s_ref, piece0, piece1, piece2, piece3, panel, diagonal):
    x = s_ref[1]
    for shift, piece in enumerate((piece0, piece1, piece2, piece3)):
        rows = pl.ds(pl.multiple_of(mod4(x - shift) * 64, 64), 64)
        panel[rows, :] = piece[:, pl.ds(0, 1152)]
        diagonal[rows, :] = piece[:, pl.ds(1152, 512)]


def wide_dot(left, panels, start, width):
    total = None
    for place, panel in enumerate(panels):
        term = jnp.dot(
            left[:, place * 256 : place * 256 + 256],
            panel[:, pl.ds(start, width)],
            preferred_element_type=F32,
        )
        total = term if total is None else total + term
    return total


def split_rows(stacked):
    width = stacked.shape[1]
    parts = stacked.reshape(4, 2, 64, width)
    return parts[:, 0].reshape(256, width), parts[:, 1].reshape(256, width)


def wide_product(left, panels, start):
    real_rows, imag_rows = split_rows(wide_dot(left, panels, start, 512))
    real = real_rows[:, :256] - imag_rows[:, 256:]
    imag = real_rows[:, 256:] + imag_rows[:, :256]
    return real, imag


def small_product(left, panels, start):
    return combine_small(*split_rows(wide_dot(left, panels, start, 128)))


def odd_kernel(s_ref, g_ref, panel0, panel1, panel2, panel3, out):
    left = g_ref[...].reshape(512, 1024)
    panels = (panel0, panel1, panel2, panel3)
    for start in (0, 512):
        real, imag = wide_product(left, panels, start)
        out[:, pl.ds(start, 256)] = real.astype(BF)
        out[:, pl.ds(start + 256, 256)] = imag.astype(BF)
    out[:, pl.ds(1024, 128)] = small_product(left, panels, 1024).astype(BF)


def even_kernel(s_ref, a_ref, c_ref, panel0, panel1, panel2, panel3, diagonal, source,
                ship, ship_lower, upper_new, diagonal_part, source_part):
    panels = (panel0, panel1, panel2, panel3)
    left = a_ref[...].reshape(512, 1024)
    ship[:, pl.ds(512, 128)] = small_product(left, panels, 1024).astype(BF)
    real, imag = wide_product(left, panels, 0)
    ship[:, pl.ds(0, 256)] = real.astype(BF)
    ship[:, pl.ds(256, 256)] = imag.astype(BF)
    real, imag = wide_product(left, panels, 512)
    ship_lower[:, pl.ds(0, 256)] = (-real).astype(BF)
    ship_lower[:, pl.ds(256, 256)] = (-imag).astype(BF)
    left = c_ref[...].reshape(512, 1024)
    own = pltpu.roll(source[:, pl.ds(1024, 128)].astype(F32), 64, 1)
    own = jnp.where(lanes_of(256) < 64, own, 0.0)
    source_part[...] = own - small_product(left, panels, 1024)
    real, imag = wide_product(left, panels, 512)
    diagonal_part[:, pl.ds(0, 256)] = diagonal[:, pl.ds(0, 256)].astype(F32) - real
    diagonal_part[:, pl.ds(256, 256)] = diagonal[:, pl.ds(256, 256)].astype(F32) - imag
    real, imag = wide_product(left, panels, 0)
    upper_new[:, pl.ds(0, 256)] = (-real).astype(BF)
    upper_new[:, pl.ds(256, 256)] = (-imag).astype(BF)


def finish_kernel(s_ref, diagonal_part, source_part, shipped, diagonal_new, source_new):
    diagonal_new[...] = (diagonal_part[...] - shipped[:, pl.ds(0, 512)].astype(F32)).astype(BF)
    source_new[...] = (source_part[...] - shipped[:, pl.ds(512, 128)].astype(F32)).astype(BF)


def pair_kernel(s_ref, lower, upper, out):
    out[:, pl.ds(0, 512)] = lower[...]
    out[:, pl.ds(512, 512)] = upper[...]


def inverse_kernel(s_ref, g_ref, base, piece0, piece1, piece2, piece3, out, add):
    left = g_ref[...].reshape(512, 1024)
    value = small_product(left, (piece0, piece1, piece2, piece3), 0)
    if add:
        value = base[...].astype(F32) + value
    out[...] = value.astype(BF)


def panel_product(block_of, pieces):
    real_rows = imag_rows = None
    for place, piece in enumerate(pieces):
        block = block_of(place)
        right = piece[...]
        real = jnp.dot(block[:, :256], right, preferred_element_type=F32)
        imag = jnp.dot(block[:, 256:512], right, preferred_element_type=F32)
        real_rows = real if real_rows is None else real_rows + real
        imag_rows = imag if imag_rows is None else imag_rows + imag
    return combine_small(real_rows, imag_rows)


def residue_kernel(s_ref, blocks, source, piece0, piece1, piece2, piece3, out):
    y = s_ref[0]
    pieces = (piece0, piece1, piece2, piece3)
    value = panel_product(lambda place: blocks[mod4(y + place)], pieces)
    out[...] = (source[...].astype(F32) - value).astype(BF)


def gather_diagonal_kernel(s_ref, block0, block1, block2, block3, out, rows_out):
    x = s_ref[1]
    rows = pl.ds(pl.multiple_of(x * 64, 64), 64)
    for shift, block in enumerate((block0, block1, block2, block3)):
        chunk = mod4(x - shift)
        out[chunk] = block[...]
        cols = pl.ds(pl.multiple_of(chunk * 256, 256), 256)
        rows_out[0, :, cols] = block[rows, pl.ds(0, 256)]
        rows_out[1, :, cols] = block[rows, pl.ds(256, 256)]


def coupling_rows_kernel(s_ref, pairs, lower_out, upper_out):
    rows = pl.ds(pl.multiple_of(s_ref[1] * 64, 64), 64)
    for chunk in range(4):
        cols = pl.ds(chunk * 256, 256)
        lower_out[0, :, cols] = pairs[chunk, rows, pl.ds(0, 256)]
        lower_out[1, :, cols] = pairs[chunk, rows, pl.ds(256, 256)]
        upper_out[0, :, cols] = pairs[chunk, rows, pl.ds(512, 256)]
        upper_out[1, :, cols] = pairs[chunk, rows, pl.ds(768, 256)]


def couple_kernel(s_ref, pairs, source, solved, piece0, piece1, piece2, piece3,
                  out0, out1, out2, out3, held):
    y, x = s_ref[0], s_ref[1]
    pieces = (piece0, piece1, piece2, piece3)
    lower = panel_product(
        lambda place: pairs[mod4(y + place), :, pl.ds(0, 512)], [p.at[0] for p in pieces]
    )
    upper = panel_product(
        lambda place: pairs[mod4(y + place), :, pl.ds(512, 512)], [p.at[1] for p in pieces]
    )
    combined = source[...].astype(F32) - lower - upper
    moved = pltpu.roll(solved[...].astype(F32), 64, 1)
    held[...] = jnp.where(lanes_of(256) < 64, combined, moved)
    for shift, out in enumerate((out0, out1, out2, out3)):
        out[...] = held[pl.ds(pl.multiple_of(mod4(x + shift) * 64, 64), 64), :]


def spread_kernel(s_ref, piece0, piece1, piece2, piece3, combined, solved):
    x = s_ref[1]
    lane = lanes_of(64)
    totals = [jnp.zeros((64, 128), F32) for _ in range(4)]
    for shift, piece in enumerate((piece0, piece1, piece2, piece3)):
        chunk = mod4(x - shift)
        value = piece[...]
        on = (lane >= chunk * 32) & (lane < chunk * 32 + 32)
        for place in range(4):
            turned = pltpu.roll(value, mod4(chunk - place) * 32, 1)
            totals[place] = jnp.where(on, turned, totals[place])
    combined[0] = totals[0]
    combined[1] = totals[1]
    solved[0] = totals[2]
    solved[1] = totals[3]


def moved_x(block, by):
    pairs = [(y * 4 + x, y * 4 + (x + by) % 4) for y in range(4) for x in range(4)]
    return lax.ppermute(block, "row", pairs)


def moved_y(block, by):
    pairs = [(y * 4 + x, ((y + by) % 4) * 4 + x) for y in range(4) for x in range(4)]
    return lax.ppermute(block, "row", pairs)


def gathered_y(block):
    return (block, moved_y(block, 3), moved_y(block, 2), moved_y(block, 1))


def gathered_x(block):
    groups = [[y * 4 + x for x in range(4)] for y in range(4)]
    return lax.all_gather(block, "row", axis_index_groups=groups)


def along_cuts(block, by):
    count = lax.axis_size("cuts")
    pairs = [(i, i + by) for i in range(count) if 0 <= i + by < count]
    return lax.ppermute(block, "cuts", pairs)


def body(diagonal_blocks, diagonal_inverses, lower_blocks, upper_blocks, injection, orbitals):
    cut = lax.axis_index("cuts")
    place = lax.axis_index("row")
    zero = jnp.zeros((1,), jnp.int32)
    window = lax.dynamic_slice_in_dim(jnp.concatenate([zero, orbitals, zero]), 2 * cut, 4)
    scalars = jnp.concatenate([jnp.stack([place // 4, place % 4]).astype(jnp.int32), window])
    pieces_and = call(
        prepare_kernel,
        [shape((64, 1664))] * 4 + [shape((2, 64, 1024))] * 4,
        0,
        scalars, diagonal_blocks, diagonal_inverses, lower_blocks, upper_blocks, injection,
    )
    pieces, (g_odd, g_even, a_even, c_even) = pieces_and[:4], pieces_and[4:]
    a_next = along_cuts(a_even, -1)
    g_odd_rows = gathered_x(g_odd)
    c_rows = gathered_x(c_even)
    a_rows = gathered_x(a_next)
    g_even_rows = gathered_x(g_even)
    pieces = [pieces[0]] + [moved_x(pieces[by], by) for by in (1, 2, 3)]
    panel, diagonal = call(
        assemble_kernel, [shape((256, 1152)), shape((256, 512))], 0, scalars, *pieces
    )
    panels = gathered_y(panel)
    (odd_panel,) = call(
        odd_kernel, [shape((256, 1152))], 2 * 512 * 1024 * 1152, scalars, g_odd_rows, *panels
    )
    odd_panels = gathered_y(odd_panel)
    ship, ship_lower, upper_new, diagonal_part, source_part = call(
        even_kernel,
        [shape((256, 640)), shape((256, 512)), shape((256, 512)), shape((256, 512), F32),
         shape((256, 128), F32)],
        4 * 512 * 1024 * 1152,
        scalars, a_rows, c_rows, *odd_panels, diagonal, panel,
    )
    shipped = along_cuts(ship, 1)
    lower_new = along_cuts(ship_lower, 1)
    diagonal_new, source = call(
        finish_kernel,
        [shape((256, 512)), shape((256, 128))],
        0, scalars, diagonal_part, source_part, shipped,
    )
    (pair,) = call(pair_kernel, [shape((256, 1024))], 0, scalars, lower_new, upper_new)
    pairs = gathered_x(pair)
    sources = gathered_y(source)
    diagonals = (diagonal_new,) + tuple(moved_x(diagonal_new, by) for by in (1, 2, 3))
    diagonal_panel, diagonal_rows = call(
        gather_diagonal_kernel,
        [shape((4, 256, 512)), shape((2, 64, 1024))],
        0, scalars, *diagonals,
    )
    solve_flops = 2 * 512 * 1024 * 128
    (iterate,) = call(
        functools.partial(inverse_kernel, add=False),
        [shape((256, 128))], solve_flops, scalars, g_even_rows, source, *sources,
    )
    for _ in range(REFINE):
        (residue,) = call(
            residue_kernel,
            [shape((256, 128))], solve_flops,
            scalars, diagonal_panel, source, *gathered_y(iterate),
        )
        (iterate,) = call(
            functools.partial(inverse_kernel, add=True),
            [shape((256, 128))], solve_flops,
            scalars, g_even_rows, iterate, *gathered_y(residue),
        )
    neighbours = jnp.stack([along_cuts(iterate, 1), along_cuts(iterate, -1)])
    ends = pl.pallas_call(
        couple_kernel,
        out_shape=tuple([shape((64, 128), F32)] * 4),
        in_specs=[SMEM] + [VMEM] * 7,
        out_specs=tuple([VMEM] * 4),
        scratch_shapes=[pltpu.VMEM((256, 128), F32)],
        compiler_params=pltpu.CompilerParams(vmem_limit_bytes=40 * 1024 * 1024),
    )(scalars, pairs, source, iterate, *gathered_y(neighbours))
    ends = [ends[0]] + [moved_x(ends[by], by) for by in (1, 2, 3)]
    combined, solved = call(
        spread_kernel, [shape((2, 64, 128), F32)] * 2, 0, scalars, *ends
    )
    lower_rows, upper_rows = call(
        coupling_rows_kernel, [shape((2, 64, 1024))] * 2, 0, scalars, pairs
    )
    return (
        diagonal_rows[None],
        lower_rows[None],
        upper_rows[None],
        combined[None],
        solved[None],
    )


def solution(mesh):
    split = P("cuts", None, "row", None)
    return jax.shard_map(
        body,
        mesh=mesh,
        in_specs=(split, split, split, split, split, P()),
        out_specs=(split,) * 5,
        check_vma=False,
    )
```

time: 462 us -> 230 us (0.50)
  the two profiles are of different devices: /device:TPU:32 before, /device:TPU:97 now
where the time goes in v1:
time: 230 us; the launch traced here: 229 us
  waiting for transfers between devices  120 us (52%)
  starting transfers between devices  58.6 us (25%)
  Pallas kernels  20.6 us (9%)
  local copies, waits for them, and re-layouts  14.9 us (6%)
  between operations  14 us (6%)
    ppermute x24, waiting for transfers between devices, moved_y(): return lax.ppermute(block, 'row', pairs)  60.5 us
    ppermute x5, starting transfers between devices, along_cuts(): return lax.ppermute(block, 'cuts', pairs)  28.5 us
    all_gather x5, waiting for transfers between devices, gathered_x(): return lax.all_gather(block, 'row', axis_index_groups=groups)  25.8 us
    pallas_call x14, Pallas kernels, call(): pl.pallas_call(kernel, out_shape=tuple(out_shapes), in_specs=[SMEM] + [VM...  19.3 us
    ppermute x5, waiting for transfers between devices, along_cuts(): return lax.ppermute(block, 'cuts', pairs)  19.2 us
    ppermute x24, starting transfers between devices, moved_y(): return lax.ppermute(block, 'row', pairs)  16 us
    unnamed x30, local copies, waits for them, and re-layouts  14.8 us
    ppermute x9, starting transfers between devices, moved_x(): return lax.ppermute(block, 'row', pairs)  14 us
  transfers between devices with their start and end apart: 43, of which 30 were waited for; matrix products, arithmetic and copies ran while one was open for 0% of the time, Pallas kernels for 7%

profile of v1, /device:TPU:97, one launch (start us, length us, event | category | flops | bytes accessed | tf_op | source)
XLA Modules:
  0.0 229.0 jit_solution(13569687592672901844)
XLA Ops:
  13.1 1.8 shard_map.101
  15.7 2.6 %collective-permute-start = (bf16[2,64,1024]{2,1,0:T(8,128)(2,1)S(1)}, bf16[2,64,1024]{2,1,0:T(8,128)(2,1)S(1)}, u32[]{:S(2)}, u32[]{:S(2)}) collective-permute-start(bf16[2,64,1024]{2,1,0:T(8,128)(2,1)S(1)} %get-tuple-element.32), channel_id=1, source_target_pairs={{16,0},{32,16},{48,32},{64,48},{80,64},{96,80},{112,96},{128,112},... | collective-permute-start | bytes 786440 | tf_op jit(solution)/shard_map/ppermute | solution.py:273
  18.3 6.8 %collective-permute-done = bf16[2,64,1024]{2,1,0:T(8,128)(2,1)S(1)} collective-permute-done((bf16[2,64,1024]{2,1,0:T(8,128)(2,1)S(1)}, bf16[2,64,1024]{2,1,0:T(8,128)(2,1)S(1)}, u32[]{:S(2)}, u32[]{:S(2)}) %collective-permute-start) | collective-permute-done | bytes 262176 | tf_op jit(solution)/shard_map/ppermute | solution.py:273
  27.2 2.5 %collective-permute-start.2 = (bf16[64,1664]{1,0:T(8,128)(2,1)S(1)}, bf16[64,1664]{1,0:T(8,128)(2,1)S(1)}, u32[]{:S(2)}, u32[]{:S(2)}) collective-permute-start(bf16[64,1664]{1,0:T(8,128)(2,1)S(1)} %get-tuple-element.37), channel_id=1, source_target_pairs={{0,2},{1,3},{2,0},{3,1},{4,6},{5,7},{6,4},{7,5},{8,10},{9,11},{10,... | collective-permute-start | bytes 638984 | tf_op jit(solution)/shard_map/ppermute | solution.py:253
  30.8 3.8 %collective-permute-done.1.piece1 = bf16[64,1664]{1,0:T(8,128)(2,1)S(1)} collective-permute-done((bf16[64,1664]{1,0:T(8,128)(2,1)S(1)}, bf16[64,1664]{1,0:T(8,128)(2,1)S(1)}, u32[]{:S(2)}, u32[]{:S(2)}) %collective-permute-start.1) | collective-permute-done | bytes 213024 | tf_op jit(solution)/shard_map/ppermute | solution.py:253
  34.5 9.2 %collective-permute-done.2.piece2 = bf16[64,1664]{1,0:T(8,128)(2,1)S(1)} collective-permute-done((bf16[64,1664]{1,0:T(8,128)(2,1)S(1)}, bf16[64,1664]{1,0:T(8,128)(2,1)S(1)}, u32[]{:S(2)}, u32[]{:S(2)}) %collective-permute-start.2) | collective-permute-done | bytes 213024 | tf_op jit(solution)/shard_map/ppermute | solution.py:253
  44.4 3.0 %collective-permute-start.4 = (bf16[256,1152]{1,0:T(8,128)(2,1)S(1)}, bf16[256,1152]{1,0:T(8,128)(2,1)S(1)}, u32[]{:S(2)}, u32[]{:S(2)}) collective-permute-start(bf16[256,1152]{1,0:T(8,128)(2,1)S(1)} %get-tuple-element.39.panel0.source), channel_id=1, source_target_pairs={{0,12},{1,13},{2,14},{3,15},{4,0},{5,1},{6,2},{7,3},{8,4},{9,5},{1... | collective-permute-start | bytes 1769480 | tf_op jit(solution)/shard_map/ppermute | solution.py:258
  48.5 22.0 %collective-permute-done.4.panel1 = bf16[256,1152]{1,0:T(8,128)(2,1)S(1)} collective-permute-done((bf16[256,1152]{1,0:T(8,128)(2,1)S(1)}, bf16[256,1152]{1,0:T(8,128)(2,1)S(1)}, u32[]{:S(2)}, u32[]{:S(2)}) %collective-permute-start.4) | collective-permute-done | bytes 589856 | tf_op jit(solution)/shard_map/ppermute | solution.py:258
  70.5 3.9 %collective-permute-done.6.panel3 = bf16[256,1152]{1,0:T(8,128)(2,1)S(1)} collective-permute-done((bf16[256,1152]{1,0:T(8,128)(2,1)S(1)}, bf16[256,1152]{1,0:T(8,128)(2,1)S(1)}, u32[]{:S(2)}, u32[]{:S(2)}) %collective-permute-start.6) | collective-permute-done | bytes 589856 | tf_op jit(solution)/shard_map/ppermute | solution.py:258
  75.6 2.1 shard_map.103.panel0
  79.3 25.8 %all-gather.11.cloned.1.call-done = bf16[8,64,1024]{2,1,0:T(8,128)(2,1)} async-done(((bf16[2,64,1024]{2,1,0:T(8,128)(2,1)}), bf16[8,64,1024]{2,1,0:T(8,128)(2,1)}) %all-gather.11.cloned.1.call-update) | async-done | bytes 1048592 | tf_op jit(solution)/shard_map/all_gather | solution.py:267
  105.1 2.7 %collective-permute-done.9.panel3 = bf16[256,1152]{1,0:T(8,128)(2,1)S(1)} collective-permute-done((bf16[256,1152]{1,0:T(8,128)(2,1)S(1)}, bf16[256,1152]{1,0:T(8,128)(2,1)S(1)}, u32[]{:S(2)}, u32[]{:S(2)}) %collective-permute-start.9) | collective-permute-done | bytes 589856 | tf_op jit(solution)/shard_map/ppermute | solution.py:258
  112.1 3.5 %shard_map.104 = (bf16[256,640]{1,0:T(8,128)(2,1)S(1)}, bf16[256,512]{1,0:T(8,128)(2,1)S(1)}, bf16[256,512]{1,0:T(8,128)(2,1)S(1)}, f32[256,512]{1,0:T(8,128)S(1)}, f32[256,128]{1,0:T(8,128)S(1)}) custom-call(s32[6]{0:T(128)S(1)} %pad_add_fusion.1.s_ref, bf16[4,2,64,1024]{3,2,1,0:T(8,128)(2,1)S(1)} %bitcast.20, bf16[4,2,64,1024]{3,2,1,0:T(8,128)(2,1)S(1)} %bitcast.19, ...), custom_call_target="tpu_custom_call" | custom-call | flops 2415919104 | bytes 6815768 | tf_op jit(solution)/shard_map/pallas_call | solution.py:21
  116.3 6.0 %collective-permute-start.14 = (bf16[256,512]{1,0:T(8,128)(2,1)S(1)}, bf16[256,512]{1,0:T(8,128)(2,1)S(1)}, u32[]{:S(2)}, u32[]{:S(2)}) collective-permute-start(bf16[256,512]{1,0:T(8,128)(2,1)S(1)} %get-tuple-element.46), channel_id=1, source_target_pairs={{0,16},{16,32},{32,48},{48,64},{64,80},{80,96},{96,112},{112,128},... | collective-permute-start | bytes 786440 | tf_op jit(solution)/shard_map/ppermute | solution.py:273
  122.3 3.3 %collective-permute-done.14.lower = bf16[256,512]{1,0:T(8,128)(2,1)S(1)} collective-permute-done((bf16[256,512]{1,0:T(8,128)(2,1)S(1)}, bf16[256,512]{1,0:T(8,128)(2,1)S(1)}, u32[]{:S(2)}, u32[]{:S(2)}) %collective-permute-start.14) | collective-permute-done | bytes 262176 | tf_op jit(solution)/shard_map/ppermute | solution.py:273
  127.0 5.6 %collective-permute-start.10 = (bf16[256,640]{1,0:T(8,128)(2,1)}, bf16[256,640]{1,0:T(8,128)(2,1)S(1)}, u32[]{:S(2)}, u32[]{:S(2)}) collective-permute-start(bf16[256,640]{1,0:T(8,128)(2,1)} %copy-done.13), channel_id=1, source_target_pairs={{0,16},{16,32},{32,48},{48,64},{64,80},{80,96},{96,112},{112,128},... | collective-permute-start | bytes 983048 | tf_op jit(solution)/shard_map/ppermute | solution.py:273
  132.7 4.3 %collective-permute-done.10.shipped = bf16[256,640]{1,0:T(8,128)(2,1)S(1)} collective-permute-done((bf16[256,640]{1,0:T(8,128)(2,1)}, bf16[256,640]{1,0:T(8,128)(2,1)S(1)}, u32[]{:S(2)}, u32[]{:S(2)}) %collective-permute-start.10) | collective-permute-done | bytes 327712 | tf_op jit(solution)/shard_map/ppermute | solution.py:273
  138.4 3.7 %collective-permute-start.12 = (bf16[256,512]{1,0:T(8,128)(2,1)S(1)}, bf16[256,512]{1,0:T(8,128)(2,1)S(1)}, u32[]{:S(2)}, u32[]{:S(2)}) collective-permute-start(bf16[256,512]{1,0:T(8,128)(2,1)S(1)} %get-tuple-element.44.block0), channel_id=1, source_target_pairs={{0,2},{1,3},{2,0},{3,1},{4,6},{5,7},{6,4},{7,5},{8,10},{9,11},{10,... | collective-permute-start | bytes 786440 | tf_op jit(solution)/shard_map/ppermute | solution.py:253
  142.1 1.8 collective-permute-start.13
  144.5 2.9 %collective-permute-done.15.piece1 = bf16[256,128]{1,0:T(8,128)(2,1)S(1)} collective-permute-done((bf16[256,128]{1,0:T(8,128)(2,1)S(1)}, bf16[256,128]{1,0:T(8,128)(2,1)S(1)}, u32[]{:S(2)}, u32[]{:S(2)}) %collective-permute-start.15) | collective-permute-done | bytes 65568 | tf_op jit(solution)/shard_map/ppermute | solution.py:258
  147.3 2.2 collective-permute-done.16.piece2
  149.6 2.1 collective-permute-done.17.piece3
  163.7 1.9 collective-permute-done.21.piece1
  165.6 2.1 collective-permute-done.22.piece2
  167.7 2.3 %collective-permute-done.23.piece3 = bf16[256,128]{1,0:T(8,128)(2,1)S(1)} collective-permute-done((bf16[256,128]{1,0:T(8,128)(2,1)S(1)}, bf16[256,128]{1,0:T(8,128)(2,1)S(1)}, u32[]{:S(2)}, u32[]{:S(2)}) %collective-permute-start.23) | collective-permute-done | bytes 65568 | tf_op jit(solution)/shard_map/ppermute | solution.py:258
  177.7 2.2 collective-permute-start.27
  181.2 3.4 %collective-permute-done.28.piece2 = bf16[256,128]{1,0:T(8,128)(2,1)S(1)} collective-permute-done((bf16[256,128]{1,0:T(8,128)(2,1)S(1)}, bf16[256,128]{1,0:T(8,128)(2,1)S(1)}, u32[]{:S(2)}, u32[]{:S(2)}) %collective-permute-start.28) | collective-permute-done | bytes 65568 | tf_op jit(solution)/shard_map/ppermute | solution.py:258
  186.2 12.3 %collective-permute-start.30 = (bf16[256,128]{1,0:T(8,128)(2,1)S(1)}, bf16[256,128]{1,0:T(8,128)(2,1)S(1)}, u32[]{:S(2)}, u32[]{:S(2)}) collective-permute-start(bf16[256,128]{1,0:T(8,128)(2,1)S(1)} %shard_map.113.solved), channel_id=1, source_target_pairs={{0,16},{16,32},{32,48},{48,64},{64,80},{80,96},{96,112},{112,128},... | collective-permute-start | bytes 196616 | tf_op jit(solution)/shard_map/ppermute | solution.py:273
  198.5 1.9 collective-permute-start.31
  200.5 4.9 %collective-permute-done.31 = bf16[256,128]{1,0:T(8,128)(2,1)S(1)} collective-permute-done((bf16[256,128]{1,0:T(8,128)(2,1)S(1)}, bf16[256,128]{1,0:T(8,128)(2,1)S(1)}, u32[]{:S(2)}, u32[]{:S(2)}) %collective-permute-start.31) | collective-permute-done | bytes 65568 | tf_op jit(solution)/shard_map/ppermute | solution.py:273
  207.3 2.2 collective-permute-done.32.piece1
  209.6 2.4 %collective-permute-done.33.piece2 = bf16[2,256,128]{2,1,0:T(8,128)(2,1)S(1)} collective-permute-done((bf16[2,256,128]{2,1,0:T(8,128)(2,1)S(1)}, bf16[2,256,128]{2,1,0:T(8,128)(2,1)S(1)}, u32[]{:S(2)}, u32[]{:S(2)}) %collective-permute-start.33) | collective-permute-done | bytes 131104 | tf_op jit(solution)/shard_map/ppermute | solution.py:258
  (108 shorter events, 58.0 us)
Async XLA Ops:
  7.2 67.2 %all-gather.15.cloned.1.call-start = ((), (), s32[]{:S(2)}) async-start(), calls=%async_computation.2 | async-start | bytes 1310720 | tf_op jit(solution)/shard_map/all_gather | solution.py:267
  14.9 64.4 %all-gather.13.cloned.1.call-start = ((), (), s32[]{:S(2)}) async-start(), calls=%async_computation.1 | async-start | bytes 1310720 | tf_op jit(solution)/shard_map/all_gather | solution.py:267
  15.7 89.4 %all-gather.11.cloned.1.call-start = ((), (), s32[]{:S(2)}) async-start(), calls=%async_computation | async-start | bytes 1310720 | tf_op jit(solution)/shard_map/all_gather | solution.py:267
  15.7 9.4 %collective-permute-start = (bf16[2,64,1024]{2,1,0:T(8,128)(2,1)S(1)}, bf16[2,64,1024]{2,1,0:T(8,128)(2,1)S(1)}, u32[]{:S(2)}, u32[]{:S(2)}) collective-permute-start(bf16[2,64,1024]{2,1,0:T(8,128)(2,1)S(1)} %get-tuple-element.32), channel_id=1, source_target_pairs={{16,0},{32,16},{48,32},{64,48},{80,64},{96,80},{112,96},{128,112},... | collective-permute-start | bytes 786440 | tf_op jit(solution)/shard_map/ppermute | solution.py:273
  25.8 121.5 %all-gather.19.cloned.1.call-start = ((), (), s32[]{:S(2)}) async-start(), calls=%async_computation.4 | async-start | bytes 1310720 | tf_op jit(solution)/shard_map/all_gather | solution.py:267
  25.9 8.7 %collective-permute-start.1 = (bf16[64,1664]{1,0:T(8,128)(2,1)S(1)}, bf16[64,1664]{1,0:T(8,128)(2,1)S(1)}, u32[]{:S(2)}, u32[]{:S(2)}) collective-permute-start(bf16[64,1664]{1,0:T(8,128)(2,1)S(1)} %get-tuple-element.36), channel_id=1, source_target_pairs={{0,1},{1,2},{2,3},{3,0},{4,5},{5,6},{6,7},{7,4},{8,9},{9,10},{10,1... | collective-permute-start | bytes 638984 | tf_op jit(solution)/shard_map/ppermute | solution.py:253
  27.2 16.6 %collective-permute-start.2 = (bf16[64,1664]{1,0:T(8,128)(2,1)S(1)}, bf16[64,1664]{1,0:T(8,128)(2,1)S(1)}, u32[]{:S(2)}, u32[]{:S(2)}) collective-permute-start(bf16[64,1664]{1,0:T(8,128)(2,1)S(1)} %get-tuple-element.37), channel_id=1, source_target_pairs={{0,2},{1,3},{2,0},{3,1},{4,6},{5,7},{6,4},{7,5},{8,10},{9,11},{10,... | collective-permute-start | bytes 638984 | tf_op jit(solution)/shard_map/ppermute | solution.py:253
  29.6 14.2 %collective-permute-start.3 = (bf16[64,1664]{1,0:T(8,128)(2,1)S(1)}, bf16[64,1664]{1,0:T(8,128)(2,1)S(1)}, u32[]{:S(2)}, u32[]{:S(2)}) collective-permute-start(bf16[64,1664]{1,0:T(8,128)(2,1)S(1)} %get-tuple-element.38), channel_id=1, source_target_pairs={{0,3},{1,0},{2,1},{3,2},{4,7},{5,4},{6,5},{7,6},{8,11},{9,8},{10,9... | collective-permute-start | bytes 638984 | tf_op jit(solution)/shard_map/ppermute | solution.py:253
  44.4 26.1 %collective-permute-start.4 = (bf16[256,1152]{1,0:T(8,128)(2,1)S(1)}, bf16[256,1152]{1,0:T(8,128)(2,1)S(1)}, u32[]{:S(2)}, u32[]{:S(2)}) collective-permute-start(bf16[256,1152]{1,0:T(8,128)(2,1)S(1)} %get-tuple-element.39.panel0.source), channel_id=1, source_target_pairs={{0,12},{1,13},{2,14},{3,15},{4,0},{5,1},{6,2},{7,3},{8,4},{9,5},{1... | collective-permute-start | bytes 1769480 | tf_op jit(solution)/shard_map/ppermute | solution.py:258
  47.5 23.0 %collective-permute-start.5 = (bf16[256,1152]{1,0:T(8,128)(2,1)S(1)}, bf16[256,1152]{1,0:T(8,128)(2,1)S(1)}, u32[]{:S(2)}, u32[]{:S(2)}) collective-permute-start(bf16[256,1152]{1,0:T(8,128)(2,1)S(1)} %get-tuple-element.39.panel0.source), channel_id=1, source_target_pairs={{0,8},{1,9},{2,10},{3,11},{4,12},{5,13},{6,14},{7,15},{8,0},{9,1},... | collective-permute-start | bytes 1769480 | tf_op jit(solution)/shard_map/ppermute | solution.py:258
  47.7 26.7 %collective-permute-start.6 = (bf16[256,1152]{1,0:T(8,128)(2,1)S(1)}, bf16[256,1152]{1,0:T(8,128)(2,1)S(1)}, u32[]{:S(2)}, u32[]{:S(2)}) collective-permute-start(bf16[256,1152]{1,0:T(8,128)(2,1)S(1)} %get-tuple-element.39.panel0.source), channel_id=1, source_target_pairs={{0,4},{1,5},{2,6},{3,7},{4,8},{5,9},{6,10},{7,11},{8,12},{9,13},{1... | collective-permute-start | bytes 1769480 | tf_op jit(solution)/shard_map/ppermute | solution.py:258
  48.4 164.8 %all-gather.17.cloned.1.call-start = ((), (), s32[]{:S(2)}) async-start(), calls=%async_computation.3 | async-start | bytes 2621440 | tf_op jit(solution)/shard_map/all_gather | solution.py:267
  77.8 27.3 %collective-permute-start.7 = (bf16[256,1152]{1,0:T(8,128)(2,1)S(1)}, bf16[256,1152]{1,0:T(8,128)(2,1)S(1)}, u32[]{:S(2)}, u32[]{:S(2)}) collective-permute-start(bf16[256,1152]{1,0:T(8,128)(2,1)S(1)} %shard_map.103.panel0), channel_id=1, source_target_pairs={{0,12},{1,13},{2,14},{3,15},{4,0},{5,1},{6,2},{7,3},{8,4},{9,5},{1... | collective-permute-start | bytes 1769480 | tf_op jit(solution)/shard_map/ppermute | solution.py:258
  78.4 26.7 %collective-permute-start.8 = (bf16[256,1152]{1,0:T(8,128)(2,1)S(1)}, bf16[256,1152]{1,0:T(8,128)(2,1)S(1)}, u32[]{:S(2)}, u32[]{:S(2)}) collective-permute-start(bf16[256,1152]{1,0:T(8,128)(2,1)S(1)} %shard_map.103.panel0), channel_id=1, source_target_pairs={{0,8},{1,9},{2,10},{3,11},{4,12},{5,13},{6,14},{7,15},{8,0},{9,1},... | collective-permute-start | bytes 1769480 | tf_op jit(solution)/shard_map/ppermute | solution.py:258
  78.5 29.2 %collective-permute-start.9 = (bf16[256,1152]{1,0:T(8,128)(2,1)S(1)}, bf16[256,1152]{1,0:T(8,128)(2,1)S(1)}, u32[]{:S(2)}, u32[]{:S(2)}) collective-permute-start(bf16[256,1152]{1,0:T(8,128)(2,1)S(1)} %shard_map.103.panel0), channel_id=1, source_target_pairs={{0,4},{1,5},{2,6},{3,7},{4,8},{5,9},{6,10},{7,11},{8,12},{9,13},{1... | collective-permute-start | bytes 1769480 | tf_op jit(solution)/shard_map/ppermute | solution.py:258
  116.3 9.3 %collective-permute-start.14 = (bf16[256,512]{1,0:T(8,128)(2,1)S(1)}, bf16[256,512]{1,0:T(8,128)(2,1)S(1)}, u32[]{:S(2)}, u32[]{:S(2)}) collective-permute-start(bf16[256,512]{1,0:T(8,128)(2,1)S(1)} %get-tuple-element.46), channel_id=1, source_target_pairs={{0,16},{16,32},{32,48},{48,64},{64,80},{80,96},{96,112},{112,128},... | collective-permute-start | bytes 786440 | tf_op jit(solution)/shard_map/ppermute | solution.py:273
  127.0 9.9 %collective-permute-start.10 = (bf16[256,640]{1,0:T(8,128)(2,1)}, bf16[256,640]{1,0:T(8,128)(2,1)S(1)}, u32[]{:S(2)}, u32[]{:S(2)}) collective-permute-start(bf16[256,640]{1,0:T(8,128)(2,1)} %copy-done.13), channel_id=1, source_target_pairs={{0,16},{16,32},{32,48},{48,64},{64,80},{80,96},{96,112},{112,128},... | collective-permute-start | bytes 983048 | tf_op jit(solution)/shard_map/ppermute | solution.py:273
  137.6 17.1 %collective-permute-start.11 = (bf16[256,512]{1,0:T(8,128)(2,1)S(1)}, bf16[256,512]{1,0:T(8,128)(2,1)S(1)}, u32[]{:S(2)}, u32[]{:S(2)}) collective-permute-start(bf16[256,512]{1,0:T(8,128)(2,1)S(1)} %get-tuple-element.44.block0), channel_id=1, source_target_pairs={{0,1},{1,2},{2,3},{3,0},{4,5},{5,6},{6,7},{7,4},{8,9},{9,10},{10,1... | collective-permute-start | bytes 786440 | tf_op jit(solution)/shard_map/ppermute | solution.py:253
  138.4 17.1 %collective-permute-start.12 = (bf16[256,512]{1,0:T(8,128)(2,1)S(1)}, bf16[256,512]{1,0:T(8,128)(2,1)S(1)}, u32[]{:S(2)}, u32[]{:S(2)}) collective-permute-start(bf16[256,512]{1,0:T(8,128)(2,1)S(1)} %get-tuple-element.44.block0), channel_id=1, source_target_pairs={{0,2},{1,3},{2,0},{3,1},{4,6},{5,7},{6,4},{7,5},{8,10},{9,11},{10,... | collective-permute-start | bytes 786440 | tf_op jit(solution)/shard_map/ppermute | solution.py:253
  142.1 13.4 %collective-permute-start.13 = (bf16[256,512]{1,0:T(8,128)(2,1)S(1)}, bf16[256,512]{1,0:T(8,128)(2,1)S(1)}, u32[]{:S(2)}, u32[]{:S(2)}) collective-permute-start(bf16[256,512]{1,0:T(8,128)(2,1)S(1)} %get-tuple-element.44.block0), channel_id=1, source_target_pairs={{0,3},{1,0},{2,1},{3,2},{4,7},{5,4},{6,5},{7,6},{8,11},{9,8},{10,9... | collective-permute-start | bytes 786440 | tf_op jit(solution)/shard_map/ppermute | solution.py:253
  144.4 5.2 %collective-permute-start.16 = (bf16[256,128]{1,0:T(8,128)(2,1)S(1)}, bf16[256,128]{1,0:T(8,128)(2,1)S(1)}, u32[]{:S(2)}, u32[]{:S(2)}) collective-permute-start(bf16[256,128]{1,0:T(8,128)(2,1)S(1)} %get-tuple-element.50.base.piece0.source), channel_id=1, source_target_pairs={{0,8},{1,9},{2,10},{3,11},{4,12},{5,13},{6,14},{7,15},{8,0},{9,1},... | collective-permute-start | bytes 196616 | tf_op jit(solution)/shard_map/ppermute | solution.py:258
  154.5 4.7 %collective-permute-start.19 = (bf16[256,128]{1,0:T(8,128)(2,1)S(1)}, bf16[256,128]{1,0:T(8,128)(2,1)S(1)}, u32[]{:S(2)}, u32[]{:S(2)}) collective-permute-start(bf16[256,128]{1,0:T(8,128)(2,1)S(1)} %shard_map.109.piece0.base), channel_id=1, source_target_pairs={{0,8},{1,9},{2,10},{3,11},{4,12},{5,13},{6,14},{7,15},{8,0},{9,1},... | collective-permute-start | bytes 196616 | tf_op jit(solution)/shard_map/ppermute | solution.py:258
  154.7 6.3 %collective-permute-start.20 = (bf16[256,128]{1,0:T(8,128)(2,1)S(1)}, bf16[256,128]{1,0:T(8,128)(2,1)S(1)}, u32[]{:S(2)}, u32[]{:S(2)}) collective-permute-start(bf16[256,128]{1,0:T(8,128)(2,1)S(1)} %shard_map.109.piece0.base), channel_id=1, source_target_pairs={{0,4},{1,5},{2,6},{3,7},{4,8},{5,9},{6,10},{7,11},{8,12},{9,13},{1... | collective-permute-start | bytes 196616 | tf_op jit(solution)/shard_map/ppermute | solution.py:258
  163.6 6.4 %collective-permute-start.23 = (bf16[256,128]{1,0:T(8,128)(2,1)S(1)}, bf16[256,128]{1,0:T(8,128)(2,1)S(1)}, u32[]{:S(2)}, u32[]{:S(2)}) collective-permute-start(bf16[256,128]{1,0:T(8,128)(2,1)S(1)} %shard_map.110.piece0), channel_id=1, source_target_pairs={{0,4},{1,5},{2,6},{3,7},{4,8},{5,9},{6,10},{7,11},{8,12},{9,13},{1... | collective-permute-start | bytes 196616 | tf_op jit(solution)/shard_map/ppermute | solution.py:258
  171.2 4.7 %collective-permute-start.25 = (bf16[256,128]{1,0:T(8,128)(2,1)S(1)}, bf16[256,128]{1,0:T(8,128)(2,1)S(1)}, u32[]{:S(2)}, u32[]{:S(2)}) collective-permute-start(bf16[256,128]{1,0:T(8,128)(2,1)S(1)} %shard_map.111.piece0.base), channel_id=1, source_target_pairs={{0,8},{1,9},{2,10},{3,11},{4,12},{5,13},{6,14},{7,15},{8,0},{9,1},... | collective-permute-start | bytes 196616 | tf_op jit(solution)/shard_map/ppermute | solution.py:258
  171.6 5.0 %collective-permute-start.26 = (bf16[256,128]{1,0:T(8,128)(2,1)S(1)}, bf16[256,128]{1,0:T(8,128)(2,1)S(1)}, u32[]{:S(2)}, u32[]{:S(2)}) collective-permute-start(bf16[256,128]{1,0:T(8,128)(2,1)S(1)} %shard_map.111.piece0.base), channel_id=1, source_target_pairs={{0,4},{1,5},{2,6},{3,7},{4,8},{5,9},{6,10},{7,11},{8,12},{9,13},{1... | collective-permute-start | bytes 196616 | tf_op jit(solution)/shard_map/ppermute | solution.py:258
  179.9 4.7 %collective-permute-start.28 = (bf16[256,128]{1,0:T(8,128)(2,1)S(1)}, bf16[256,128]{1,0:T(8,128)(2,1)S(1)}, u32[]{:S(2)}, u32[]{:S(2)}) collective-permute-start(bf16[256,128]{1,0:T(8,128)(2,1)S(1)} %shard_map.112.piece0), channel_id=1, source_target_pairs={{0,8},{1,9},{2,10},{3,11},{4,12},{5,13},{6,14},{7,15},{8,0},{9,1},... | collective-permute-start | bytes 196616 | tf_op jit(solution)/shard_map/ppermute | solution.py:258
  180.1 5.0 %collective-permute-start.29 = (bf16[256,128]{1,0:T(8,128)(2,1)S(1)}, bf16[256,128]{1,0:T(8,128)(2,1)S(1)}, u32[]{:S(2)}, u32[]{:S(2)}) collective-permute-start(bf16[256,128]{1,0:T(8,128)(2,1)S(1)} %shard_map.112.piece0), channel_id=1, source_target_pairs={{0,4},{1,5},{2,6},{3,7},{4,8},{5,9},{6,10},{7,11},{8,12},{9,13},{1... | collective-permute-start | bytes 196616 | tf_op jit(solution)/shard_map/ppermute | solution.py:258
  186.2 14.3 %collective-permute-start.30 = (bf16[256,128]{1,0:T(8,128)(2,1)S(1)}, bf16[256,128]{1,0:T(8,128)(2,1)S(1)}, u32[]{:S(2)}, u32[]{:S(2)}) collective-permute-start(bf16[256,128]{1,0:T(8,128)(2,1)S(1)} %shard_map.113.solved), channel_id=1, source_target_pairs={{0,16},{16,32},{32,48},{48,64},{64,80},{80,96},{96,112},{112,128},... | collective-permute-start | bytes 196616 | tf_op jit(solution)/shard_map/ppermute | solution.py:273
  198.5 6.8 %collective-permute-start.31 = (bf16[256,128]{1,0:T(8,128)(2,1)S(1)}, bf16[256,128]{1,0:T(8,128)(2,1)S(1)}, u32[]{:S(2)}, u32[]{:S(2)}) collective-permute-start(bf16[256,128]{1,0:T(8,128)(2,1)S(1)} %shard_map.113.solved), channel_id=1, source_target_pairs={{16,0},{32,16},{48,32},{64,48},{80,64},{96,80},{112,96},{128,112},... | collective-permute-start | bytes 196616 | tf_op jit(solution)/shard_map/ppermute | solution.py:273
  206.5 5.4 %collective-permute-start.33 = (bf16[2,256,128]{2,1,0:T(8,128)(2,1)S(1)}, bf16[2,256,128]{2,1,0:T(8,128)(2,1)S(1)}, u32[]{:S(2)}, u32[]{:S(2)}) collective-permute-start(bf16[2,256,128]{2,1,0:T(8,128)(2,1)S(1)} %pad_maximum_fusion.piece0), channel_id=1, source_target_pairs={{0,8},{1,9},{2,10},{3,11},{4,12},{5,13},{6,14},{7,15},{8,0},{9,1},... | collective-permute-start | bytes 393224 | tf_op jit(solution)/shard_map/ppermute | solution.py:258
  207.1 6.1 %collective-permute-start.34 = (bf16[2,256,128]{2,1,0:T(8,128)(2,1)S(1)}, bf16[2,256,128]{2,1,0:T(8,128)(2,1)S(1)}, u32[]{:S(2)}, u32[]{:S(2)}) collective-permute-start(bf16[2,256,128]{2,1,0:T(8,128)(2,1)S(1)} %pad_maximum_fusion.piece0), channel_id=1, source_target_pairs={{0,4},{1,5},{2,6},{3,7},{4,8},{5,9},{6,10},{7,11},{8,12},{9,13},{1... | collective-permute-start | bytes 393224 | tf_op jit(solution)/shard_map/ppermute | solution.py:258
  (26 other events, 75.6 us)
Sparse Core Ops, SparseCore 0:
  15.1 32.1 all-gather.14
  49.7 26.6 all-gather.12
  78.2 26.8 all-gather.10
  107.3 26.8 all-gather.18
  135.9 34.6 all-gather.16

commit v2 on v1

v2 whole, which is shorter than its diff:
```python
import functools

import jax
import jax.numpy as jnp
from jax import lax
from jax.experimental import pallas as pl
from jax.experimental.pallas import tpu as pltpu
from jax.sharding import PartitionSpec as P

REFINE = 2
BF = jnp.bfloat16
F32 = jnp.float32
VMEM = pl.BlockSpec(memory_space=pltpu.VMEM)
SMEM = pl.BlockSpec(memory_space=pltpu.SMEM)


def call(kernel, out_shapes, flops, *args, scratch=(), hbm=0):
    moved = sum(a.size * a.dtype.itemsize for a in args) + sum(
        s.size * s.dtype.itemsize for s in out_shapes
    )
    anywhere = pl.BlockSpec(memory_space=pl.ANY)
    return pl.pallas_call(
        kernel,
        out_shape=tuple(out_shapes),
        in_specs=[SMEM] + [anywhere] * hbm + [VMEM] * (len(args) - 1 - hbm),
        out_specs=tuple([VMEM] * len(out_shapes)),
        scratch_shapes=list(scratch),
        compiler_params=pltpu.CompilerParams(vmem_limit_bytes=32 * 1024 * 1024),
        cost_estimate=pl.CostEstimate(flops=flops, bytes_accessed=moved, transcendentals=0),
    )(*args)


def shape(dims, dtype=BF):
    return jax.ShapeDtypeStruct(dims, dtype)


def mod4(v):
    return lax.rem(v + 8, 4)


def at(chunk, size):
    return pl.ds(pl.multiple_of(chunk * size, size), size)


def lanes_of(rows):
    return lax.broadcasted_iota(jnp.int32, (rows, 128), 1)


def combine_small(real_rows, imag_rows):
    lane = lanes_of(real_rows.shape[0])
    turned = jnp.where(lane < 32, -pltpu.roll(imag_rows, 96, 1), pltpu.roll(imag_rows, 32, 1))
    return jnp.where(lane < 64, real_rows + turned, 0.0)


def packed(block):
    half = block.shape[0] // 2
    return jnp.where(lanes_of(half) < 64, block[:half], pltpu.roll(block[half:], 64, 1))


def halves(block):
    return block, pltpu.roll(block, 64, 1)


def masked(block, first_row, rows_on, chunk, cols_on):
    row = first_row + lax.broadcasted_iota(jnp.int32, (64, 256), 0)
    col = chunk * 256 + lax.broadcasted_iota(jnp.int32, (64, 256), 1)
    return jnp.where((row < rows_on) & (col < cols_on), block.astype(F32), 0.0).astype(BF)


def prepare_kernel(s_ref, d_hbm, a_hbm, c_hbm, b_hbm, piece0, piece1, piece2, piece3,
                   d_ref, a_ref, c_ref, b_ref, sems):
    y, x = s_ref[0], s_ref[1]
    first_row = (y * 4 + x) * 64
    before, own, odd, after = s_ref[2], s_ref[3], s_ref[4], s_ref[5]
    copies = [
        pltpu.make_async_copy(source, target, sems.at[index])
        for index, (source, target) in enumerate(
            (
                (c_hbm.at[1, 0], c_ref.at[0]),
                (c_hbm.at[1, 1], c_ref.at[1]),
                (b_hbm, b_ref),
                (a_hbm.at[1, 0], a_ref.at[0]),
                (a_hbm.at[1, 1], a_ref.at[1]),
                (d_hbm.at[0, 0], d_ref.at[0]),
                (d_hbm.at[0, 1], d_ref.at[1]),
            )
        )
    ]
    for copy in copies:
        copy.start()
    pieces = (piece0, piece1, piece2, piece3)
    row_b = first_row + lax.broadcasted_iota(jnp.int32, (64, 128), 0)
    lane = lanes_of(64)
    copies[0].wait()
    copies[1].wait()
    for shift, piece in enumerate(pieces):
        chunk = mod4(x + shift)
        for part in range(2):
            piece[:, pl.ds(part * 256, 256)] = masked(
                c_ref[part, :, at(chunk, 256)], first_row, odd, chunk, after
            )
    copies[2].wait()
    blocks = [
        jnp.where(row_b < rows_on, b_ref[which, part].astype(F32), 0.0)
        for which, part, rows_on in ((1, 0, odd), (1, 1, odd), (0, 0, own), (0, 1, own))
    ]
    for shift, piece in enumerate(pieces):
        chunk = mod4(x + shift)
        tile = jnp.zeros((64, 128), F32)
        for place, block in enumerate(blocks):
            turned = pltpu.roll(block, mod4(place - chunk) * 32, 1)
            tile = jnp.where((lane >= place * 32) & (lane < place * 32 + 32), turned, tile)
        piece[:, pl.ds(512, 128)] = tile.astype(BF)
    copies[3].wait()
    copies[4].wait()
    for shift, piece in enumerate(pieces):
        chunk = mod4(x + shift)
        for part in range(2):
            piece[:, pl.ds(640 + part * 256, 256)] = masked(
                a_ref[part, :, at(chunk, 256)], first_row, odd, chunk, own
            )
    copies[5].wait()
    copies[6].wait()
    for shift, piece in enumerate(pieces):
        chunk = mod4(x + shift)
        for part in range(2):
            piece[:, pl.ds(1152 + part * 256, 256)] = d_ref[part, :, at(chunk, 256)]


def couplings_kernel(s_ref, a_ref, c_ref, a_even, c_even):
    first_row = (s_ref[0] * 4 + s_ref[1]) * 64
    before, own, odd = s_ref[2], s_ref[3], s_ref[4]
    for chunk in range(4):
        cols = pl.ds(chunk * 256, 256)
        for part in range(2):
            a_even[part, :, cols] = masked(a_ref[part, :, cols], first_row, own, chunk, before)
            c_even[part, :, cols] = masked(c_ref[part, :, cols], first_row, own, chunk, odd)


def assemble_kernel(s_ref, piece0, piece1, piece2, piece3, panel, panel_a, diagonal):
    x = s_ref[1]
    for shift, piece in enumerate((piece0, piece1, piece2, piece3)):
        rows = at(mod4(x - shift), 64)
        panel[rows, :] = piece[:, pl.ds(0, 640)]
        panel_a[rows, :] = piece[:, pl.ds(640, 512)]
        diagonal[rows, :] = piece[:, pl.ds(1152, 512)]


def stack_rows(x, blocks, held):
    for shift, block in enumerate(blocks):
        held[at(mod4(x - shift), 128), :] = block[...].reshape(128, 1024)


def wide_dot(y, held, panels, start, width):
    total = None
    for place, panel in enumerate(panels):
        term = jnp.dot(
            held[:, at(mod4(y + place), 256)],
            panel[:, pl.ds(start, width)],
            preferred_element_type=F32,
        )
        total = term if total is None else total + term
    parts = total.reshape(4, 2, 64, width)
    return parts[:, 0].reshape(256, width), parts[:, 1].reshape(256, width)


def wide_product(y, held, panels):
    real_rows, imag_rows = wide_dot(y, held, panels, 0, 512)
    real = real_rows[:, :256] - imag_rows[:, 256:]
    imag = real_rows[:, 256:] + imag_rows[:, :256]
    return real, imag


def small_product(y, held, panels):
    return combine_small(*wide_dot(y, held, panels, 512, 128))


def put_pair(out, real, imag):
    out[:, pl.ds(0, 256)] = real.astype(out.dtype)
    out[:, pl.ds(256, 256)] = imag.astype(out.dtype)


def odd_kernel(s_ref, g0, g1, g2, g3, panel0, panel1, panel2, panel3, out, g_rows, held):
    y, x = s_ref[0], s_ref[1]
    panels = (panel0, panel1, panel2, panel3)
    stack_rows(x, (g0, g1, g2, g3), held)
    g_rows[...] = held[...]
    put_pair(out, *wide_product(y, held, panels))
    out[:, pl.ds(512, 128)] = small_product(y, held, panels).astype(BF)


def odd_second_kernel(s_ref, g_rows, panel0, panel1, panel2, panel3, out):
    put_pair(out, *wide_product(s_ref[0], g_rows, (panel0, panel1, panel2, panel3)))


def even_kernel(s_ref, ca0, ca1, ca2, ca3, panel0, panel1, panel2, panel3, source,
                ship, upper_new, source_part, a_rows, c_rows):
    y, x = s_ref[0], s_ref[1]
    panels = (panel0, panel1, panel2, panel3)
    blocks = (ca0, ca1, ca2, ca3)
    stack_rows(x, [b.at[1] for b in blocks], a_rows)
    stack_rows(x, [b.at[0] for b in blocks], c_rows)
    ship[:, pl.ds(512, 128)] = small_product(y, a_rows, panels).astype(BF)
    put_pair(ship, *wide_product(y, a_rows, panels))
    own = pltpu.roll(source[:, pl.ds(512, 128)].astype(F32), 64, 1)
    own = jnp.where(lanes_of(256) < 64, own, 0.0)
    source_part[...] = own - small_product(y, c_rows, panels)
    real, imag = wide_product(y, c_rows, panels)
    put_pair(upper_new, -real, -imag)


def source_kernel(s_ref, source_part, shipped, source_new):
    source_new[...] = packed(
        source_part[...] - shipped[:, pl.ds(512, 128)].astype(F32)
    ).astype(BF)


def diagonal_kernel(s_ref, c_rows, panel0, panel1, panel2, panel3, diagonal, shipped, out):
    real, imag = wide_product(s_ref[0], c_rows, (panel0, panel1, panel2, panel3))
    real = diagonal[:, pl.ds(0, 256)].astype(F32) - real - shipped[:, pl.ds(0, 256)].astype(F32)
    imag = diagonal[:, pl.ds(256, 256)].astype(F32) - imag - shipped[:, pl.ds(256, 256)].astype(F32)
    put_pair(out, real, imag)


def lower_kernel(s_ref, a_rows, panel0, panel1, panel2, panel3, out):
    real, imag = wide_product(s_ref[0], a_rows, (panel0, panel1, panel2, panel3))
    put_pair(out, -real, -imag)


def pair_kernel(s_ref, lower, upper, out):
    out[:, pl.ds(0, 512)] = lower[...]
    out[:, pl.ds(512, 512)] = upper[...]


def whole_inverse(y, g_ref, pieces, vector):
    for place, piece in enumerate(pieces):
        for index, half in enumerate(halves(piece[...].astype(F32))):
            rows = pl.ds(pl.multiple_of(mod4(y + place) * 256 + index * 128, 128), 128)
            vector[rows, :] = half.astype(BF)
    right = vector[...]
    for block in range(4):
        left = g_ref[pl.ds(block * 4, 4)].reshape(512, 1024)
        total = jnp.dot(left, right, preferred_element_type=F32).reshape(4, 2, 64, 128)
        yield block, combine_small(
            total[:, 0].reshape(256, 128), total[:, 1].reshape(256, 128)
        )


def solve_kernel(s_ref, g_ref, piece0, piece1, piece2, piece3, out, vector):
    pieces = (piece0, piece1, piece2, piece3)
    for block, value in whole_inverse(s_ref[0], g_ref, pieces, vector):
        out[pl.ds(block * 256, 256), :] = value.astype(BF)


def block_product(block, right):
    real = jnp.dot(block[:, pl.ds(0, 256)], right, preferred_element_type=F32)
    imag = jnp.dot(block[:, pl.ds(256, 256)], right, preferred_element_type=F32)
    return real, imag


def residue_of(x, blocks, source, solved):
    real_rows = imag_rows = None
    for shift, block in enumerate(blocks):
        real, imag = block_product(block, solved[at(mod4(x - shift), 256), :])
        real_rows = real if real_rows is None else real_rows + real
        imag_rows = imag if imag_rows is None else imag_rows + imag
    value = packed(combine_small(real_rows, imag_rows))
    return (source[...].astype(F32) - value).astype(BF)


def residue_kernel(s_ref, block0, block1, block2, block3, source, solved, out):
    out[...] = residue_of(s_ref[1], (block0, block1, block2, block3), source, solved)


def turn_kernel(s_ref, g_ref, piece0, piece1, piece2, piece3, solved,
                block0, block1, block2, block3, source, out, residue, vector):
    pieces = (piece0, piece1, piece2, piece3)
    for block, value in whole_inverse(s_ref[0], g_ref, pieces, vector):
        rows = pl.ds(block * 256, 256)
        out[rows, :] = (solved[rows, :].astype(F32) + value).astype(BF)
    residue[...] = residue_of(s_ref[1], (block0, block1, block2, block3), source, out)


def last_kernel(s_ref, g_ref, piece0, piece1, piece2, piece3, solved, out, ship, vector):
    pieces = (piece0, piece1, piece2, piece3)
    for block, value in whole_inverse(s_ref[0], g_ref, pieces, vector):
        rows = pl.ds(block * 256, 256)
        out[rows, :] = (solved[rows, :].astype(F32) + value).astype(BF)
    ship[...] = packed(out[...].astype(F32)).astype(BF)


def diagonal_rows_kernel(s_ref, block0, block1, block2, block3, rows_out):
    x = s_ref[1]
    rows = at(x, 64)
    for shift, block in enumerate((block0, block1, block2, block3)):
        cols = at(mod4(x - shift), 256)
        rows_out[0, :, cols] = block[rows, pl.ds(0, 256)]
        rows_out[1, :, cols] = block[rows, pl.ds(256, 256)]


def coupling_rows_kernel(s_ref, pairs, lower_out, upper_out):
    rows = at(s_ref[1], 64)
    for chunk in range(4):
        cols = pl.ds(chunk * 256, 256)
        lower_out[0, :, cols] = pairs[chunk, rows, pl.ds(0, 256)]
        lower_out[1, :, cols] = pairs[chunk, rows, pl.ds(256, 256)]
        upper_out[0, :, cols] = pairs[chunk, rows, pl.ds(512, 256)]
        upper_out[1, :, cols] = pairs[chunk, rows, pl.ds(768, 256)]


def coupled(pairs, start, neighbour):
    parts = []
    for half in range(2):
        real_rows = imag_rows = None
        for index in range(2):
            block = pairs.at[half * 2 + index, :, pl.ds(start, 512)]
            real, imag = block_product(block, neighbour[pl.ds(index * 256, 256), :])
            real_rows = real if real_rows is None else real_rows + real
            imag_rows = imag if imag_rows is None else imag_rows + imag
        parts.append((real_rows, imag_rows))
    real_rows = parts[0][0] + pltpu.roll(parts[1][0], 64, 1)
    imag_rows = parts[0][1] + pltpu.roll(parts[1][1], 64, 1)
    return combine_small(real_rows, imag_rows)


def couple_kernel(s_ref, pairs, source, solved, below, above, out0, out1, out2, out3, held):
    y, x = s_ref[0], s_ref[1]
    combined = -coupled(pairs, 0, below) - coupled(pairs, 512, above)
    for index, half in enumerate(halves(source[...].astype(F32))):
        rows = pl.ds(index * 128, 128)
        moved = pltpu.roll(
            solved[pl.ds(pl.multiple_of(y * 256 + index * 128, 128), 128), :].astype(F32), 64, 1
        )
        total = half + combined[index * 128 : index * 128 + 128]
        held[rows, :] = jnp.where(lanes_of(128) < 64, total, moved)
    for shift, out in enumerate((out0, out1, out2, out3)):
        out[...] = held[at(mod4(x + shift), 64), :]


def spread_kernel(s_ref, piece0, piece1, piece2, piece3, combined, solved):
    x = s_ref[1]
    lane = lanes_of(64)
    totals = [jnp.zeros((64, 128), F32) for _ in range(4)]
    for shift, piece in enumerate((piece0, piece1, piece2, piece3)):
        chunk = mod4(x - shift)
        value = piece[...]
        on = (lane >= chunk * 32) & (lane < chunk * 32 + 32)
        for place in range(4):
            turned = pltpu.roll(value, mod4(chunk - place) * 32, 1)
            totals[place] = jnp.where(on, turned, totals[place])
    combined[0] = totals[0]
    combined[1] = totals[1]
    solved[0] = totals[2]
    solved[1] = totals[3]


def moved_x(block, by):
    pairs = [(y * 4 + x, y * 4 + (x + by) % 4) for y in range(4) for x in range(4)]
    return lax.ppermute(block, "row", pairs)


def moved_y(block, by):
    pairs = [(y * 4 + x, ((y + by) % 4) * 4 + x) for y in range(4) for x in range(4)]
    return lax.ppermute(block, "row", pairs)


def gathered_y(block):
    return (block, moved_y(block, 3), moved_y(block, 2), moved_y(block, 1))


def gathered_x(block):
    groups = [[y * 4 + x for x in range(4)] for y in range(4)]
    return lax.all_gather(block, "row", axis_index_groups=groups)


def along_cuts(block, by):
    count = lax.axis_size("cuts")
    pairs = [(i, i + by) for i in range(count) if 0 <= i + by < count]
    return lax.ppermute(block, "cuts", pairs)


def body(diagonal_blocks, diagonal_inverses, lower_blocks, upper_blocks, injection, orbitals):
    cut = lax.axis_index("cuts")
    place = lax.axis_index("row")
    zero = jnp.zeros((1,), jnp.int32)
    window = lax.dynamic_slice_in_dim(jnp.concatenate([zero, orbitals, zero]), 2 * cut, 4)
    scalars = jnp.concatenate([jnp.stack([place // 4, place % 4]).astype(jnp.int32), window])
    turns = (1, 2, 3)
    wide_flops = 2 * 512 * 1024 * 512
    solve_flops = 2 * 2048 * 1024 * 128
    vector = pltpu.VMEM((1024, 128), BF)

    pieces = call(
        prepare_kernel,
        [shape((64, 1664))] * 4,
        0,
        scalars, diagonal_blocks, lower_blocks, upper_blocks, injection,
        hbm=4,
        scratch=[pltpu.VMEM((2, 64, 1024), BF)] * 3
        + [pltpu.VMEM((2, 2, 64, 128), BF), pltpu.SemaphoreType.DMA((7,))],
    )
    inverse_even = lax.all_gather(diagonal_inverses[0], "row")
    pieces = [pieces[0]] + [moved_x(pieces[by], by) for by in turns]
    a_even, c_even = call(
        couplings_kernel,
        [shape((2, 64, 1024))] * 2,
        0,
        scalars, lower_blocks[0], upper_blocks[0],
    )
    couplings = jnp.stack([c_even, along_cuts(a_even, -1)])
    g_odd = diagonal_inverses[1]
    g_blocks = [g_odd] + [moved_x(g_odd, by) for by in turns]
    panel, panel_a, diagonal = call(
        assemble_kernel,
        [shape((256, 640)), shape((256, 512)), shape((256, 512))],
        0, scalars, *pieces,
    )
    panels = gathered_y(panel)
    panels_a = gathered_y(panel_a)
    ca_blocks = [couplings] + [moved_x(couplings, by) for by in turns]
    first, g_rows = call(
        odd_kernel, [shape((256, 640)), shape((512, 1024))], wide_flops,
        scalars, *g_blocks, *panels, scratch=[pltpu.VMEM((512, 1024), BF)],
    )
    firsts = gathered_y(first)
    (second,) = call(
        odd_second_kernel, [shape((256, 512))], wide_flops, scalars, g_rows, *panels_a
    )
    seconds = gathered_y(second)
    ship, upper_new, source_part, a_rows, c_rows = call(
        even_kernel,
        [shape((256, 640)), shape((256, 512)), shape((256, 128), F32), shape((512, 1024)),
         shape((512, 1024))],
        2 * wide_flops,
        scalars, *ca_blocks, *firsts, panel,
    )
    shipped = along_cuts(ship, 1)
    (source,) = call(source_kernel, [shape((128, 128))], 0, scalars, source_part, shipped)
    sources = gathered_y(source)
    (diagonal_new,) = call(
        diagonal_kernel, [shape((256, 512))], wide_flops,
        scalars, c_rows, *seconds, diagonal, shipped,
    )
    diagonals = [diagonal_new] + [moved_x(diagonal_new, by) for by in turns]
    (ship_lower,) = call(
        lower_kernel, [shape((256, 512))], wide_flops, scalars, a_rows, *seconds
    )
    lower_new = along_cuts(ship_lower, 1)
    (pair,) = call(pair_kernel, [shape((256, 1024))], 0, scalars, lower_new, upper_new)
    pairs = gathered_x(pair)
    (solved,) = call(
        solve_kernel, [shape((1024, 128))], solve_flops,
        scalars, inverse_even, *sources, scratch=[vector],
    )
    (residue,) = call(
        residue_kernel, [shape((128, 128))], solve_flops // 4,
        scalars, *diagonals, source, solved,
    )
    for _ in range(REFINE - 1):
        solved, residue = call(
            turn_kernel, [shape((1024, 128)), shape((128, 128))], solve_flops,
            scalars, inverse_even, *gathered_y(residue), solved, *diagonals, source,
            scratch=[vector],
        )
    solved, ship_solved = call(
        last_kernel, [shape((1024, 128)), shape((512, 128))], solve_flops,
        scalars, inverse_even, *gathered_y(residue), solved, scratch=[vector],
    )
    below, above = along_cuts(ship_solved, 1), along_cuts(ship_solved, -1)
    (diagonal_rows,) = call(
        diagonal_rows_kernel, [shape((2, 64, 1024))], 0, scalars, *diagonals
    )
    lower_rows, upper_rows = call(
        coupling_rows_kernel, [shape((2, 64, 1024))] * 2, 0, scalars, pairs
    )
    ends = call(
        couple_kernel, [shape((64, 128), F32)] * 4, solve_flops // 2,
        scalars, pairs, source, solved, below, above,
        scratch=[pltpu.VMEM((256, 128), F32)],
    )
    ends = [ends[0]] + [moved_x(ends[by], by) for by in turns]
    combined, solved_rows = call(
        spread_kernel, [shape((2, 64, 128), F32)] * 2, 0, scalars, *ends
    )
    return (
        diagonal_rows[None],
        lower_rows[None],
        upper_rows[None],
        combined[None],
        solved_rows[None],
    )


def solution(mesh):
    split = P("cuts", None, "row", None)
    return jax.shard_map(
        body,
        mesh=mesh,
        in_specs=(split, split, split, split, split, P()),
        out_specs=(split,) * 5,
        check_vma=False,
    )
```

time: 230 us -> 216 us (0.939)
  waiting for transfers between devices: 120 us -> 102 us
  Pallas kernels: 20.6 us -> 26.3 us
  local copies, waits for them, and re-layouts: 14.9 us -> 9.66 us
  starting transfers between devices: 58.6 us -> 62 us
    all_gather x5 -> x1, waiting for transfers between devices: 25.8 us -> 0.02 us  [gathered_x(): return lax.all_gather(block, 'row', axis_index_groups=groups)]
    ppermute x9 -> x15, waiting for transfers between devices: 13.8 us -> 28.8 us  [moved_x(): return lax.ppermute(block, 'row', pairs)]
    ppermute x24 -> x21, starting transfers between devices: 16 us -> 25.2 us  [moved_y(): return lax.ppermute(block, 'row', pairs)]
    unnamed x30 -> x16, local copies, waits for them, and re-layouts: 14.8 us -> 7.77 us
    ppermute x5, waiting for transfers between devices: 19.2 us -> 12.8 us  [along_cuts(): return lax.ppermute(block, 'cuts', pairs)]
    pallas_call x15 -> x18, Pallas kernels: 20.6 us -> 26.3 us  [call(): pl.pallas_call(kernel, out_shape=tuple(out_shapes), in_specs=[SMEM] + [an...]
    ppermute x5, starting transfers between devices: 28.5 us -> 24 us  [along_cuts(): return lax.ppermute(block, 'cuts', pairs)]
    ppermute x9 -> x15, starting transfers between devices: 14 us -> 12.6 us  [moved_x(): return lax.ppermute(block, 'row', pairs)]
  transfers between devices with their start and end apart: 43 -> 43, of which waited for: 30 -> 24; matrix products, arithmetic and copies ran while one was open for 0% -> 0% of each run, Pallas kernels for 7% -> 11%
where the time goes in v2:
time: 216 us; the launch traced here: 215 us
  waiting for transfers between devices  102 us (47%)
  starting transfers between devices  62 us (29%)
  Pallas kernels  26.3 us (12%)
  between operations  14.3 us (7%)
  local copies, waits for them, and re-layouts  9.66 us (4%)
    ppermute x21, waiting for transfers between devices, moved_y(): return lax.ppermute(block, 'row', pairs)  60.3 us
    ppermute x15, waiting for transfers between devices, moved_x(): return lax.ppermute(block, 'row', pairs)  28.8 us
    pallas_call x18, Pallas kernels, call(): pl.pallas_call(kernel, out_shape=tuple(out_shapes), in_specs=[SMEM] + [an...  26.3 us
    ppermute x21, starting transfers between devices, moved_y(): return lax.ppermute(block, 'row', pairs)  25.2 us
    ppermute x5, starting transfers between devices, along_cuts(): return lax.ppermute(block, 'cuts', pairs)  24 us
    ppermute x5, waiting for transfers between devices, along_cuts(): return lax.ppermute(block, 'cuts', pairs)  12.8 us
    ppermute x15, starting transfers between devices, moved_x(): return lax.ppermute(block, 'row', pairs)  12.6 us
    unnamed x16, local copies, waits for them, and re-layouts  7.77 us
  transfers between devices with their start and end apart: 43, of which 24 were waited for; matrix products, arithmetic and copies ran while one was open for 0% of the time, Pallas kernels for 11%

profile of v2, /device:TPU:97, one launch (start us, length us, event | category | flops | bytes accessed | tf_op | source)
XLA Modules:
  0.0 215.1 jit_solution(15376403756504539194)
XLA Ops:
  17.2 2.5 %collective-permute-start.8 = (bf16[64,1664]{1,0:T(8,128)(2,1)S(1)}, bf16[64,1664]{1,0:T(8,128)(2,1)S(1)}, u32[]{:S(2)}, u32[]{:S(2)}) collective-permute-start(bf16[64,1664]{1,0:T(8,128)(2,1)S(1)} %get-tuple-element.37), channel_id=1, source_target_pairs={{0,2},{1,3},{2,0},{3,1},{4,6},{5,7},{6,4},{7,5},{8,10},{9,11},{10,... | collective-permute-start | bytes 638984 | tf_op jit(solution)/shard_map/ppermute | solution.py:359
  20.4 3.1 %collective-permute-start = (bf16[2,64,1024]{2,1,0:T(8,128)(2,1)S(1)}, bf16[2,64,1024]{2,1,0:T(8,128)(2,1)S(1)}, u32[]{:S(2)}, u32[]{:S(2)}) collective-permute-start(bf16[2,64,1024]{2,1,0:T(8,128)(2,1)S(1)} %get-tuple-element.34), channel_id=1, source_target_pairs={{16,0},{32,16},{48,32},{64,48},{80,64},{96,80},{112,96},{128,112},... | collective-permute-start | bytes 786440 | tf_op jit(solution)/shard_map/ppermute | solution.py:379
  23.7 2.3 %collective-permute-start.5 = (bf16[2,64,1024]{2,1,0:T(8,128)(2,1)S(1)}, bf16[2,64,1024]{2,1,0:T(8,128)(2,1)S(1)}, u32[]{:S(2)}, u32[]{:S(2)}) collective-permute-start(bf16[2,64,1024]{2,1,0:T(8,128)(2,1)S(1)} %get-tuple-element.62.g0), channel_id=1, source_target_pairs={{0,2},{1,3},{2,0},{3,1},{4,6},{5,7},{6,4},{7,5},{8,10},{9,11},{10,... | collective-permute-start | bytes 786440 | tf_op jit(solution)/shard_map/ppermute | solution.py:359
  26.3 2.6 %collective-permute-done.8.piece2 = bf16[64,1664]{1,0:T(8,128)(2,1)S(1)} collective-permute-done((bf16[64,1664]{1,0:T(8,128)(2,1)S(1)}, bf16[64,1664]{1,0:T(8,128)(2,1)S(1)}, u32[]{:S(2)}, u32[]{:S(2)}) %collective-permute-start.8) | collective-permute-done | bytes 213024 | tf_op jit(solution)/shard_map/ppermute | solution.py:359
  28.9 13.4 %collective-permute-done.9.piece3 = bf16[64,1664]{1,0:T(8,128)(2,1)S(1)} collective-permute-done((bf16[64,1664]{1,0:T(8,128)(2,1)S(1)}, bf16[64,1664]{1,0:T(8,128)(2,1)S(1)}, u32[]{:S(2)}, u32[]{:S(2)}) %collective-permute-start.9) | collective-permute-done | bytes 213024 | tf_op jit(solution)/shard_map/ppermute | solution.py:359
  43.0 3.0 %collective-permute-start.10 = (bf16[256,640]{1,0:T(8,128)(2,1)S(1)}, bf16[256,640]{1,0:T(8,128)(2,1)S(1)}, u32[]{:S(2)}, u32[]{:S(2)}) collective-permute-start(bf16[256,640]{1,0:T(8,128)(2,1)S(1)} %get-tuple-element.39.panel0.source), channel_id=1, source_target_pairs={{0,12},{1,13},{2,14},{3,15},{4,0},{5,1},{6,2},{7,3},{8,4},{9,5},{1... | collective-permute-start | bytes 983048 | tf_op jit(solution)/shard_map/ppermute | solution.py:364
  48.1 14.1 %collective-permute-done.16.panel1 = bf16[256,512]{1,0:T(8,128)(2,1)S(1)} collective-permute-done((bf16[256,512]{1,0:T(8,128)(2,1)S(1)}, bf16[256,512]{1,0:T(8,128)(2,1)S(1)}, u32[]{:S(2)}, u32[]{:S(2)}) %collective-permute-start.16) | collective-permute-done | bytes 262176 | tf_op jit(solution)/shard_map/ppermute | solution.py:364
  62.7 7.5 %collective-permute-done.12.panel3 = bf16[256,640]{1,0:T(8,128)(2,1)S(1)} collective-permute-done((bf16[256,640]{1,0:T(8,128)(2,1)S(1)}, bf16[256,640]{1,0:T(8,128)(2,1)S(1)}, u32[]{:S(2)}, u32[]{:S(2)}) %collective-permute-start.12) | collective-permute-done | bytes 327712 | tf_op jit(solution)/shard_map/ppermute | solution.py:364
  70.2 3.2 %collective-permute-start.18 = (bf16[256,512]{1,0:T(8,128)(2,1)S(1)}, bf16[256,512]{1,0:T(8,128)(2,1)S(1)}, u32[]{:S(2)}, u32[]{:S(2)}) collective-permute-start(bf16[256,512]{1,0:T(8,128)(2,1)S(1)} %get-tuple-element.43.panel0), channel_id=1, source_target_pairs={{0,4},{1,5},{2,6},{3,7},{4,8},{5,9},{6,10},{7,11},{8,12},{9,13},{1... | collective-permute-start | bytes 786440 | tf_op jit(solution)/shard_map/ppermute | solution.py:364
  75.1 2.4 %collective-permute-done.17.panel2 = bf16[256,512]{1,0:T(8,128)(2,1)S(1)} collective-permute-done((bf16[256,512]{1,0:T(8,128)(2,1)S(1)}, bf16[256,512]{1,0:T(8,128)(2,1)S(1)}, u32[]{:S(2)}, u32[]{:S(2)}) %collective-permute-start.17) | collective-permute-done | bytes 262176 | tf_op jit(solution)/shard_map/ppermute | solution.py:364
  77.5 5.7 %collective-permute-start.13 = (bf16[256,640]{1,0:T(8,128)(2,1)S(1)}, bf16[256,640]{1,0:T(8,128)(2,1)S(1)}, u32[]{:S(2)}, u32[]{:S(2)}) collective-permute-start(bf16[256,640]{1,0:T(8,128)(2,1)S(1)} %get-tuple-element.40.panel0), channel_id=1, source_target_pairs={{0,12},{1,13},{2,14},{3,15},{4,0},{5,1},{6,2},{7,3},{8,4},{9,5},{1... | collective-permute-start | bytes 983048 | tf_op jit(solution)/shard_map/ppermute | solution.py:364
  83.2 4.3 %collective-permute-done.18.panel3 = bf16[256,512]{1,0:T(8,128)(2,1)S(1)} collective-permute-done((bf16[256,512]{1,0:T(8,128)(2,1)S(1)}, bf16[256,512]{1,0:T(8,128)(2,1)S(1)}, u32[]{:S(2)}, u32[]{:S(2)}) %collective-permute-start.18) | collective-permute-done | bytes 262176 | tf_op jit(solution)/shard_map/ppermute | solution.py:364
  92.4 2.1 collective-permute-done.3.ca3
  94.5 2.7 %collective-permute-start.20 = (bf16[256,512]{1,0:T(8,128)(2,1)S(1)}, bf16[256,512]{1,0:T(8,128)(2,1)S(1)}, u32[]{:S(2)}, u32[]{:S(2)}) collective-permute-start(bf16[256,512]{1,0:T(8,128)(2,1)S(1)} %shard_map.106.panel0), channel_id=1, source_target_pairs={{0,8},{1,9},{2,10},{3,11},{4,12},{5,13},{6,14},{7,15},{8,0},{9,1},... | collective-permute-start | bytes 786440 | tf_op jit(solution)/shard_map/ppermute | solution.py:364
  98.6 10.1 %collective-permute-done.15.panel3 = bf16[256,640]{1,0:T(8,128)(2,1)S(1)} collective-permute-done((bf16[256,640]{1,0:T(8,128)(2,1)S(1)}, bf16[256,640]{1,0:T(8,128)(2,1)S(1)}, u32[]{:S(2)}, u32[]{:S(2)}) %collective-permute-start.15) | collective-permute-done | bytes 327712 | tf_op jit(solution)/shard_map/ppermute | solution.py:364
  108.7 2.4 %shard_map.105 = (bf16[256,640]{1,0:T(8,128)(2,1)S(1)}, bf16[256,512]{1,0:T(8,128)(2,1)S(1)}, f32[256,128]{1,0:T(8,128)S(1)}, bf16[512,1024]{1,0:T(8,128)(2,1)S(1)}, bf16[512,1024]{1,0:T(8,128)(2,1)S(1)}) custom-call(s32[6]{0:T(128)S(1)} %pad_add_fusion.1.s_ref, bf16[2,2,64,1024]{3,2,1,0:T(8,128)(2,1)S(1)} %pad_maximum_fusion.ca0, ...), custom_call_target="tpu_custom_call" | custom-call | flops 1073741824 | bytes 6553624 | tf_op jit(solution)/shard_map/pallas_call | solution.py:22
  111.2 6.1 %collective-permute-done.21.panel3 = bf16[256,512]{1,0:T(8,128)(2,1)S(1)} collective-permute-done((bf16[256,512]{1,0:T(8,128)(2,1)S(1)}, bf16[256,512]{1,0:T(8,128)(2,1)S(1)}, u32[]{:S(2)}, u32[]{:S(2)}) %collective-permute-start.21) | collective-permute-done | bytes 262176 | tf_op jit(solution)/shard_map/ppermute | solution.py:364
  118.5 5.5 %collective-permute-start.26 = (bf16[256,512]{1,0:T(8,128)(2,1)S(1)}, bf16[256,512]{1,0:T(8,128)(2,1)S(1)}, u32[]{:S(2)}, u32[]{:S(2)}) collective-permute-start(bf16[256,512]{1,0:T(8,128)(2,1)S(1)} %shard_map.109), channel_id=1, source_target_pairs={{0,16},{16,32},{32,48},{48,64},{64,80},{80,96},{96,112},{112,128},... | collective-permute-start | bytes 786440 | tf_op jit(solution)/shard_map/ppermute | solution.py:379
  124.1 3.3 %collective-permute-done.26.lower = bf16[256,512]{1,0:T(8,128)(2,1)S(1)} collective-permute-done((bf16[256,512]{1,0:T(8,128)(2,1)S(1)}, bf16[256,512]{1,0:T(8,128)(2,1)S(1)}, u32[]{:S(2)}, u32[]{:S(2)}) %collective-permute-start.26) | collective-permute-done | bytes 262176 | tf_op jit(solution)/shard_map/ppermute | solution.py:379
  128.7 5.6 %collective-permute-start.22 = (bf16[256,640]{1,0:T(8,128)(2,1)S(1)}, bf16[256,640]{1,0:T(8,128)(2,1)S(1)}, u32[]{:S(2)}, u32[]{:S(2)}) collective-permute-start(bf16[256,640]{1,0:T(8,128)(2,1)S(1)} %get-tuple-element.45), channel_id=1, source_target_pairs={{0,16},{16,32},{32,48},{48,64},{64,80},{80,96},{96,112},{112,128},... | collective-permute-start | bytes 983048 | tf_op jit(solution)/shard_map/ppermute | solution.py:379
  134.4 4.0 %collective-permute-done.22.shipped = bf16[256,640]{1,0:T(8,128)(2,1)S(1)} collective-permute-done((bf16[256,640]{1,0:T(8,128)(2,1)S(1)}, bf16[256,640]{1,0:T(8,128)(2,1)S(1)}, u32[]{:S(2)}, u32[]{:S(2)}) %collective-permute-start.22) | collective-permute-done | bytes 327712 | tf_op jit(solution)/shard_map/ppermute | solution.py:379
  139.8 2.2 collective-permute-start.24
  143.9 2.7 %collective-permute-done.27.piece1 = bf16[128,128]{1,0:T(8,128)(2,1)S(1)} collective-permute-done((bf16[128,128]{1,0:T(8,128)(2,1)S(1)}, bf16[128,128]{1,0:T(8,128)(2,1)S(1)}, u32[]{:S(2)}, u32[]{:S(2)}) %collective-permute-start.27) | collective-permute-done | bytes 32800 | tf_op jit(solution)/shard_map/ppermute | solution.py:364
  148.2 2.8 %collective-permute-done.29.piece3 = bf16[128,128]{1,0:T(8,128)(2,1)S(1)} collective-permute-done((bf16[128,128]{1,0:T(8,128)(2,1)S(1)}, bf16[128,128]{1,0:T(8,128)(2,1)S(1)}, u32[]{:S(2)}, u32[]{:S(2)}) %collective-permute-start.29) | collective-permute-done | bytes 32800 | tf_op jit(solution)/shard_map/ppermute | solution.py:364
  151.0 2.2 %copy-done = bf16[16,2,64,1024]{3,2,1,0:T(8,128)(2,1)S(1)} copy-done((bf16[16,2,64,1024]{3,2,1,0:T(8,128)(2,1)S(1)}, bf16[16,2,64,1024]{3,2,1,0:T(8,128)(2,1)}, u32[]{:S(2)}) %copy-start) | copy-done | bytes 4194328
  155.2 9.4 %collective-permute-done.24.block2 = bf16[256,512]{1,0:T(8,128)(2,1)S(1)} collective-permute-done((bf16[256,512]{1,0:T(8,128)(2,1)S(1)}, bf16[256,512]{1,0:T(8,128)(2,1)S(1)}, u32[]{:S(2)}, u32[]{:S(2)}) %collective-permute-start.24) | collective-permute-done | bytes 262176 | tf_op jit(solution)/shard_map/ppermute | solution.py:359
  170.0 2.5 %collective-permute-done.31.piece2 = bf16[128,128]{1,0:T(8,128)(2,1)S(1)} collective-permute-done((bf16[128,128]{1,0:T(8,128)(2,1)S(1)}, bf16[128,128]{1,0:T(8,128)(2,1)S(1)}, u32[]{:S(2)}, u32[]{:S(2)}) %collective-permute-start.31) | collective-permute-done | bytes 32800 | tf_op jit(solution)/shard_map/ppermute | solution.py:364
  173.2 2.5 %shard_map.115 = (bf16[1024,128]{1,0:T(8,128)(2,1)S(1)}, bf16[128,128]{1,0:T(8,128)(2,1)S(1)}) custom-call(s32[6]{0:T(128)S(1)} %pad_add_fusion.1.s_ref, bf16[16,2,64,1024]{3,2,1,0:T(8,128)(2,1)S(1)} %copy-done.1, bf16[128,128]{1,0:T(8,128)(2,1)S(1)} %shard_map.114.piece0, bf16[128,128]{1,0:T(8,128)(2,1)S(1)} %collective-permute-done.30.piece1, ...), custom_call_target="tpu_custom_call" | custom-call | flops 536870912 | bytes 5963800 | tf_op jit(solution)/shard_map/pallas_call | solution.py:22
  181.0 2.0 shard_map.116
  183.0 7.9 %collective-permute-start.36 = (bf16[512,128]{1,0:T(8,128)(2,1)S(1)}, bf16[512,128]{1,0:T(8,128)(2,1)S(1)}, u32[]{:S(2)}, u32[]{:S(2)}) collective-permute-start(bf16[512,128]{1,0:T(8,128)(2,1)S(1)} %get-tuple-element.54), channel_id=1, source_target_pairs={{0,16},{16,32},{32,48},{48,64},{64,80},{80,96},{96,112},{112,128},... | collective-permute-start | bytes 393224 | tf_op jit(solution)/shard_map/ppermute | solution.py:379
  192.8 5.5 %collective-permute-done.37.above = bf16[512,128]{1,0:T(8,128)(2,1)S(1)} collective-permute-done((bf16[512,128]{1,0:T(8,128)(2,1)S(1)}, bf16[512,128]{1,0:T(8,128)(2,1)S(1)}, u32[]{:S(2)}, u32[]{:S(2)}) %collective-permute-start.37) | collective-permute-done | bytes 131104 | tf_op jit(solution)/shard_map/ppermute | solution.py:379
  201.6 2.6 %collective-permute-start.40 = (f32[64,128]{1,0:T(8,128)S(1)}, f32[64,128]{1,0:T(8,128)S(1)}, u32[]{:S(2)}, u32[]{:S(2)}) collective-permute-start(f32[64,128]{1,0:T(8,128)S(1)} %get-tuple-element.58), channel_id=1, source_target_pairs={{0,3},{1,0},{2,1},{3,2},{4,7},{5,4},{6,5},{7,6},{8,11},{9,8},{10,9... | collective-permute-start | bytes 98312 | tf_op jit(solution)/shard_map/ppermute | solution.py:359
  (96 shorter events, 52.3 us)
Async XLA Ops:
  7.2 143.8 %all-gather.4.cloned.1.call-start = ((), (), s32[]{:S(2)}) async-start(), calls=%async_computation | async-start | bytes 4456448 | tf_op jit(solution)/shard_map/all_gather | solution.py:402
  9.0 183.8 %all-gather.6.cloned.1.call-start = ((), (), s32[]{:S(2)}) async-start(), calls=%async_computation.1 | async-start | bytes 2621440 | tf_op jit(solution)/shard_map/all_gather | solution.py:373
  16.0 10.0 %collective-permute-start.7 = (bf16[64,1664]{1,0:T(8,128)(2,1)S(1)}, bf16[64,1664]{1,0:T(8,128)(2,1)S(1)}, u32[]{:S(2)}, u32[]{:S(2)}) collective-permute-start(bf16[64,1664]{1,0:T(8,128)(2,1)S(1)} %get-tuple-element.36), channel_id=1, source_target_pairs={{0,1},{1,2},{2,3},{3,0},{4,5},{5,6},{6,7},{7,4},{8,9},{9,10},{10,1... | collective-permute-start | bytes 638984 | tf_op jit(solution)/shard_map/ppermute | solution.py:359
  17.2 11.7 %collective-permute-start.8 = (bf16[64,1664]{1,0:T(8,128)(2,1)S(1)}, bf16[64,1664]{1,0:T(8,128)(2,1)S(1)}, u32[]{:S(2)}, u32[]{:S(2)}) collective-permute-start(bf16[64,1664]{1,0:T(8,128)(2,1)S(1)} %get-tuple-element.37), channel_id=1, source_target_pairs={{0,2},{1,3},{2,0},{3,1},{4,6},{5,7},{6,4},{7,5},{8,10},{9,11},{10,... | collective-permute-start | bytes 638984 | tf_op jit(solution)/shard_map/ppermute | solution.py:359
  20.4 25.6 %collective-permute-start = (bf16[2,64,1024]{2,1,0:T(8,128)(2,1)S(1)}, bf16[2,64,1024]{2,1,0:T(8,128)(2,1)S(1)}, u32[]{:S(2)}, u32[]{:S(2)}) collective-permute-start(bf16[2,64,1024]{2,1,0:T(8,128)(2,1)S(1)} %get-tuple-element.34), channel_id=1, source_target_pairs={{16,0},{32,16},{48,32},{64,48},{80,64},{96,80},{112,96},{128,112},... | collective-permute-start | bytes 786440 | tf_op jit(solution)/shard_map/ppermute | solution.py:379
  23.6 22.9 %collective-permute-start.4 = (bf16[2,64,1024]{2,1,0:T(8,128)(2,1)S(1)}, bf16[2,64,1024]{2,1,0:T(8,128)(2,1)S(1)}, u32[]{:S(2)}, u32[]{:S(2)}) collective-permute-start(bf16[2,64,1024]{2,1,0:T(8,128)(2,1)S(1)} %get-tuple-element.62.g0), channel_id=1, source_target_pairs={{0,1},{1,2},{2,3},{3,0},{4,5},{5,6},{6,7},{7,4},{8,9},{9,10},{10,1... | collective-permute-start | bytes 786440 | tf_op jit(solution)/shard_map/ppermute | solution.py:359
  23.7 22.8 %collective-permute-start.5 = (bf16[2,64,1024]{2,1,0:T(8,128)(2,1)S(1)}, bf16[2,64,1024]{2,1,0:T(8,128)(2,1)S(1)}, u32[]{:S(2)}, u32[]{:S(2)}) collective-permute-start(bf16[2,64,1024]{2,1,0:T(8,128)(2,1)S(1)} %get-tuple-element.62.g0), channel_id=1, source_target_pairs={{0,2},{1,3},{2,0},{3,1},{4,6},{5,7},{6,4},{7,5},{8,10},{9,11},{10,... | collective-permute-start | bytes 786440 | tf_op jit(solution)/shard_map/ppermute | solution.py:359
  26.0 16.4 %collective-permute-start.9 = (bf16[64,1664]{1,0:T(8,128)(2,1)S(1)}, bf16[64,1664]{1,0:T(8,128)(2,1)S(1)}, u32[]{:S(2)}, u32[]{:S(2)}) collective-permute-start(bf16[64,1664]{1,0:T(8,128)(2,1)S(1)} %get-tuple-element.38), channel_id=1, source_target_pairs={{0,3},{1,0},{2,1},{3,2},{4,7},{5,4},{6,5},{7,6},{8,11},{9,8},{10,9... | collective-permute-start | bytes 638984 | tf_op jit(solution)/shard_map/ppermute | solution.py:359
  28.9 18.9 %collective-permute-start.6 = (bf16[2,64,1024]{2,1,0:T(8,128)(2,1)S(1)}, bf16[2,64,1024]{2,1,0:T(8,128)(2,1)S(1)}, u32[]{:S(2)}, u32[]{:S(2)}) collective-permute-start(bf16[2,64,1024]{2,1,0:T(8,128)(2,1)S(1)} %get-tuple-element.62.g0), channel_id=1, source_target_pairs={{0,3},{1,0},{2,1},{3,2},{4,7},{5,4},{6,5},{7,6},{8,11},{9,8},{10,9... | collective-permute-start | bytes 786440 | tf_op jit(solution)/shard_map/ppermute | solution.py:359
  43.0 19.2 %collective-permute-start.10 = (bf16[256,640]{1,0:T(8,128)(2,1)S(1)}, bf16[256,640]{1,0:T(8,128)(2,1)S(1)}, u32[]{:S(2)}, u32[]{:S(2)}) collective-permute-start(bf16[256,640]{1,0:T(8,128)(2,1)S(1)} %get-tuple-element.39.panel0.source), channel_id=1, source_target_pairs={{0,12},{1,13},{2,14},{3,15},{4,0},{5,1},{6,2},{7,3},{8,4},{9,5},{1... | collective-permute-start | bytes 983048 | tf_op jit(solution)/shard_map/ppermute | solution.py:364
  46.0 16.2 %collective-permute-start.16 = (bf16[256,512]{1,0:T(8,128)(2,1)S(1)}, bf16[256,512]{1,0:T(8,128)(2,1)S(1)}, u32[]{:S(2)}, u32[]{:S(2)}) collective-permute-start(bf16[256,512]{1,0:T(8,128)(2,1)S(1)} %get-tuple-element.43.panel0), channel_id=1, source_target_pairs={{0,12},{1,13},{2,14},{3,15},{4,0},{5,1},{6,2},{7,3},{8,4},{9,5},{1... | collective-permute-start | bytes 786440 | tf_op jit(solution)/shard_map/ppermute | solution.py:364
  46.4 15.8 %collective-permute-start.11 = (bf16[256,640]{1,0:T(8,128)(2,1)S(1)}, bf16[256,640]{1,0:T(8,128)(2,1)S(1)}, u32[]{:S(2)}, u32[]{:S(2)}) collective-permute-start(bf16[256,640]{1,0:T(8,128)(2,1)S(1)} %get-tuple-element.39.panel0.source), channel_id=1, source_target_pairs={{0,8},{1,9},{2,10},{3,11},{4,12},{5,13},{6,14},{7,15},{8,0},{9,1},... | collective-permute-start | bytes 983048 | tf_op jit(solution)/shard_map/ppermute | solution.py:364
  46.4 23.7 %collective-permute-start.12 = (bf16[256,640]{1,0:T(8,128)(2,1)S(1)}, bf16[256,640]{1,0:T(8,128)(2,1)S(1)}, u32[]{:S(2)}, u32[]{:S(2)}) collective-permute-start(bf16[256,640]{1,0:T(8,128)(2,1)S(1)} %get-tuple-element.39.panel0.source), channel_id=1, source_target_pairs={{0,4},{1,5},{2,6},{3,7},{4,8},{5,9},{6,10},{7,11},{8,12},{9,13},{1... | collective-permute-start | bytes 983048 | tf_op jit(solution)/shard_map/ppermute | solution.py:364
  47.9 40.5 %collective-permute-start.1 = (bf16[2,2,64,1024]{3,2,1,0:T(8,128)(2,1)S(1)}, bf16[2,2,64,1024]{3,2,1,0:T(8,128)(2,1)S(1)}, u32[]{:S(2)}, u32[]{:S(2)}) collective-permute-start(bf16[2,2,64,1024]{3,2,1,0:T(8,128)(2,1)S(1)} %pad_maximum_fusion.ca0), channel_id=1, source_target_pairs={{0,1},{1,2},{2,3},{3,0},{4,5},{5,6},{6,7},{7,4},{8,9},{9,10},{10,1... | collective-permute-start | bytes 1572872 | tf_op jit(solution)/shard_map/ppermute | solution.py:359
  62.2 15.3 %collective-permute-start.17 = (bf16[256,512]{1,0:T(8,128)(2,1)S(1)}, bf16[256,512]{1,0:T(8,128)(2,1)S(1)}, u32[]{:S(2)}, u32[]{:S(2)}) collective-permute-start(bf16[256,512]{1,0:T(8,128)(2,1)S(1)} %get-tuple-element.43.panel0), channel_id=1, source_target_pairs={{0,8},{1,9},{2,10},{3,11},{4,12},{5,13},{6,14},{7,15},{8,0},{9,1},... | collective-permute-start | bytes 786440 | tf_op jit(solution)/shard_map/ppermute | solution.py:364
  62.2 28.8 %collective-permute-start.2 = (bf16[2,2,64,1024]{3,2,1,0:T(8,128)(2,1)S(1)}, bf16[2,2,64,1024]{3,2,1,0:T(8,128)(2,1)S(1)}, u32[]{:S(2)}, u32[]{:S(2)}) collective-permute-start(bf16[2,2,64,1024]{3,2,1,0:T(8,128)(2,1)S(1)} %pad_maximum_fusion.ca0), channel_id=1, source_target_pairs={{0,2},{1,3},{2,0},{3,1},{4,6},{5,7},{6,4},{7,5},{8,10},{9,11},{10,... | collective-permute-start | bytes 1572872 | tf_op jit(solution)/shard_map/ppermute | solution.py:359
  62.2 32.3 %collective-permute-start.3 = (bf16[2,2,64,1024]{3,2,1,0:T(8,128)(2,1)S(1)}, bf16[2,2,64,1024]{3,2,1,0:T(8,128)(2,1)S(1)}, u32[]{:S(2)}, u32[]{:S(2)}) collective-permute-start(bf16[2,2,64,1024]{3,2,1,0:T(8,128)(2,1)S(1)} %pad_maximum_fusion.ca0), channel_id=1, source_target_pairs={{0,3},{1,0},{2,1},{3,2},{4,7},{5,4},{6,5},{7,6},{8,11},{9,8},{10,9... | collective-permute-start | bytes 1572872 | tf_op jit(solution)/shard_map/ppermute | solution.py:359
  70.2 17.4 %collective-permute-start.18 = (bf16[256,512]{1,0:T(8,128)(2,1)S(1)}, bf16[256,512]{1,0:T(8,128)(2,1)S(1)}, u32[]{:S(2)}, u32[]{:S(2)}) collective-permute-start(bf16[256,512]{1,0:T(8,128)(2,1)S(1)} %get-tuple-element.43.panel0), channel_id=1, source_target_pairs={{0,4},{1,5},{2,6},{3,7},{4,8},{5,9},{6,10},{7,11},{8,12},{9,13},{1... | collective-permute-start | bytes 786440 | tf_op jit(solution)/shard_map/ppermute | solution.py:364
  77.5 19.7 %collective-permute-start.13 = (bf16[256,640]{1,0:T(8,128)(2,1)S(1)}, bf16[256,640]{1,0:T(8,128)(2,1)S(1)}, u32[]{:S(2)}, u32[]{:S(2)}) collective-permute-start(bf16[256,640]{1,0:T(8,128)(2,1)S(1)} %get-tuple-element.40.panel0), channel_id=1, source_target_pairs={{0,12},{1,13},{2,14},{3,15},{4,0},{5,1},{6,2},{7,3},{8,4},{9,5},{1... | collective-permute-start | bytes 983048 | tf_op jit(solution)/shard_map/ppermute | solution.py:364
  87.5 11.0 %collective-permute-start.14 = (bf16[256,640]{1,0:T(8,128)(2,1)S(1)}, bf16[256,640]{1,0:T(8,128)(2,1)S(1)}, u32[]{:S(2)}, u32[]{:S(2)}) collective-permute-start(bf16[256,640]{1,0:T(8,128)(2,1)S(1)} %get-tuple-element.40.panel0), channel_id=1, source_target_pairs={{0,8},{1,9},{2,10},{3,11},{4,12},{5,13},{6,14},{7,15},{8,0},{9,1},... | collective-permute-start | bytes 983048 | tf_op jit(solution)/shard_map/ppermute | solution.py:364
  88.4 20.3 %collective-permute-start.15 = (bf16[256,640]{1,0:T(8,128)(2,1)S(1)}, bf16[256,640]{1,0:T(8,128)(2,1)S(1)}, u32[]{:S(2)}, u32[]{:S(2)}) collective-permute-start(bf16[256,640]{1,0:T(8,128)(2,1)S(1)} %get-tuple-element.40.panel0), channel_id=1, source_target_pairs={{0,4},{1,5},{2,6},{3,7},{4,8},{5,9},{6,10},{7,11},{8,12},{9,13},{1... | collective-permute-start | bytes 983048 | tf_op jit(solution)/shard_map/ppermute | solution.py:364
  91.0 20.1 %collective-permute-start.19 = (bf16[256,512]{1,0:T(8,128)(2,1)S(1)}, bf16[256,512]{1,0:T(8,128)(2,1)S(1)}, u32[]{:S(2)}, u32[]{:S(2)}) collective-permute-start(bf16[256,512]{1,0:T(8,128)(2,1)S(1)} %shard_map.106.panel0), channel_id=1, source_target_pairs={{0,12},{1,13},{2,14},{3,15},{4,0},{5,1},{6,2},{7,3},{8,4},{9,5},{1... | collective-permute-start | bytes 786440 | tf_op jit(solution)/shard_map/ppermute | solution.py:364
  94.5 16.6 %collective-permute-start.20 = (bf16[256,512]{1,0:T(8,128)(2,1)S(1)}, bf16[256,512]{1,0:T(8,128)(2,1)S(1)}, u32[]{:S(2)}, u32[]{:S(2)}) collective-permute-start(bf16[256,512]{1,0:T(8,128)(2,1)S(1)} %shard_map.106.panel0), channel_id=1, source_target_pairs={{0,8},{1,9},{2,10},{3,11},{4,12},{5,13},{6,14},{7,15},{8,0},{9,1},... | collective-permute-start | bytes 786440 | tf_op jit(solution)/shard_map/ppermute | solution.py:364
  97.2 20.1 %collective-permute-start.21 = (bf16[256,512]{1,0:T(8,128)(2,1)S(1)}, bf16[256,512]{1,0:T(8,128)(2,1)S(1)}, u32[]{:S(2)}, u32[]{:S(2)}) collective-permute-start(bf16[256,512]{1,0:T(8,128)(2,1)S(1)} %shard_map.106.panel0), channel_id=1, source_target_pairs={{0,4},{1,5},{2,6},{3,7},{4,8},{5,9},{6,10},{7,11},{8,12},{9,13},{1... | collective-permute-start | bytes 786440 | tf_op jit(solution)/shard_map/ppermute | solution.py:364
  118.5 8.8 %collective-permute-start.26 = (bf16[256,512]{1,0:T(8,128)(2,1)S(1)}, bf16[256,512]{1,0:T(8,128)(2,1)S(1)}, u32[]{:S(2)}, u32[]{:S(2)}) collective-permute-start(bf16[256,512]{1,0:T(8,128)(2,1)S(1)} %shard_map.109), channel_id=1, source_target_pairs={{0,16},{16,32},{32,48},{48,64},{64,80},{80,96},{96,112},{112,128},... | collective-permute-start | bytes 786440 | tf_op jit(solution)/shard_map/ppermute | solution.py:379
  128.7 9.6 %collective-permute-start.22 = (bf16[256,640]{1,0:T(8,128)(2,1)S(1)}, bf16[256,640]{1,0:T(8,128)(2,1)S(1)}, u32[]{:S(2)}, u32[]{:S(2)}) collective-permute-start(bf16[256,640]{1,0:T(8,128)(2,1)S(1)} %get-tuple-element.45), channel_id=1, source_target_pairs={{0,16},{16,32},{32,48},{48,64},{64,80},{80,96},{96,112},{112,128},... | collective-permute-start | bytes 983048 | tf_op jit(solution)/shard_map/ppermute | solution.py:379
  139.6 15.6 %collective-permute-start.23 = (bf16[256,512]{1,0:T(8,128)(2,1)S(1)}, bf16[256,512]{1,0:T(8,128)(2,1)S(1)}, u32[]{:S(2)}, u32[]{:S(2)}) collective-permute-start(bf16[256,512]{1,0:T(8,128)(2,1)S(1)} %shard_map.107.block0), channel_id=1, source_target_pairs={{0,1},{1,2},{2,3},{3,0},{4,5},{5,6},{6,7},{7,4},{8,9},{9,10},{10,1... | collective-permute-start | bytes 786440 | tf_op jit(solution)/shard_map/ppermute | solution.py:359
  139.8 24.8 %collective-permute-start.24 = (bf16[256,512]{1,0:T(8,128)(2,1)S(1)}, bf16[256,512]{1,0:T(8,128)(2,1)S(1)}, u32[]{:S(2)}, u32[]{:S(2)}) collective-permute-start(bf16[256,512]{1,0:T(8,128)(2,1)S(1)} %shard_map.107.block0), channel_id=1, source_target_pairs={{0,2},{1,3},{2,0},{3,1},{4,6},{5,7},{6,4},{7,5},{8,10},{9,11},{10,... | collective-permute-start | bytes 786440 | tf_op jit(solution)/shard_map/ppermute | solution.py:359
  142.0 23.6 %collective-permute-start.25 = (bf16[256,512]{1,0:T(8,128)(2,1)S(1)}, bf16[256,512]{1,0:T(8,128)(2,1)S(1)}, u32[]{:S(2)}, u32[]{:S(2)}) collective-permute-start(bf16[256,512]{1,0:T(8,128)(2,1)S(1)} %shard_map.107.block0), channel_id=1, source_target_pairs={{0,3},{1,0},{2,1},{3,2},{4,7},{5,4},{6,5},{7,6},{8,11},{9,8},{10,9... | collective-permute-start | bytes 786440 | tf_op jit(solution)/shard_map/ppermute | solution.py:359
  167.7 5.5 %collective-permute-start.32 = (bf16[128,128]{1,0:T(8,128)(2,1)S(1)}, bf16[128,128]{1,0:T(8,128)(2,1)S(1)}, u32[]{:S(2)}, u32[]{:S(2)}) collective-permute-start(bf16[128,128]{1,0:T(8,128)(2,1)S(1)} %shard_map.114.piece0), channel_id=1, source_target_pairs={{0,4},{1,5},{2,6},{3,7},{4,8},{5,9},{6,10},{7,11},{8,12},{9,13},{1... | collective-permute-start | bytes 98312 | tf_op jit(solution)/shard_map/ppermute | solution.py:364
  183.0 9.8 %collective-permute-start.36 = (bf16[512,128]{1,0:T(8,128)(2,1)S(1)}, bf16[512,128]{1,0:T(8,128)(2,1)S(1)}, u32[]{:S(2)}, u32[]{:S(2)}) collective-permute-start(bf16[512,128]{1,0:T(8,128)(2,1)S(1)} %get-tuple-element.54), channel_id=1, source_target_pairs={{0,16},{16,32},{32,48},{48,64},{64,80},{80,96},{96,112},{112,128},... | collective-permute-start | bytes 393224 | tf_op jit(solution)/shard_map/ppermute | solution.py:379
  190.9 7.5 %collective-permute-start.37 = (bf16[512,128]{1,0:T(8,128)(2,1)S(1)}, bf16[512,128]{1,0:T(8,128)(2,1)S(1)}, u32[]{:S(2)}, u32[]{:S(2)}) collective-permute-start(bf16[512,128]{1,0:T(8,128)(2,1)S(1)} %get-tuple-element.54), channel_id=1, source_target_pairs={{16,0},{32,16},{48,32},{64,48},{80,64},{96,80},{112,96},{128,112},... | collective-permute-start | bytes 393224 | tf_op jit(solution)/shard_map/ppermute | solution.py:379
  (19 other events, 81.5 us)
Sparse Core Ops, SparseCore 0:
  11.0 86.3 all-gather.3
  128.9 42.4 all-gather.5

commit v3 on v2

--- a/solution.py
+++ b/solution.py
@@ -14,7 +14,7 @@
 SMEM = pl.BlockSpec(memory_space=pltpu.SMEM)
 
 
-def call(kernel, out_shapes, flops, *args, scratch=(), hbm=0):
+def call(kernel, out_shapes, flops, *args, scratch=(), hbm=0, mib=32):
     moved = sum(a.size * a.dtype.itemsize for a in args) + sum(
         s.size * s.dtype.itemsize for s in out_shapes
     )
@@ -25,7 +25,7 @@
         in_specs=[SMEM] + [anywhere] * hbm + [VMEM] * (len(args) - 1 - hbm),
         out_specs=tuple([VMEM] * len(out_shapes)),
         scratch_shapes=list(scratch),
-        compiler_params=pltpu.CompilerParams(vmem_limit_bytes=32 * 1024 * 1024),
+        compiler_params=pltpu.CompilerParams(vmem_limit_bytes=mib * 1024 * 1024),
         cost_estimate=pl.CostEstimate(flops=flops, bytes_accessed=moved, transcendentals=0),
     )(*args)
 
@@ -67,8 +67,9 @@
     return jnp.where((row < rows_on) & (col < cols_on), block.astype(F32), 0.0).astype(BF)
 
 
-def prepare_kernel(s_ref, d_hbm, a_hbm, c_hbm, b_hbm, piece0, piece1, piece2, piece3,
-                   d_ref, a_ref, c_ref, b_ref, sems):
+def prepare_kernel(s_ref, d_hbm, g_hbm, a_hbm, c_hbm, b_hbm, piece0, piece1, piece2, piece3,
+                   a_even, c_even, g0, g1, g2, g3,
+                   d_ref, a_ref, c_ref, b_ref, a_first, c_first, g_first, sems):
     y, x = s_ref[0], s_ref[1]
     first_row = (y * 4 + x) * 64
     before, own, odd, after = s_ref[2], s_ref[3], s_ref[4], s_ref[5]
@@ -83,6 +84,9 @@
                 (a_hbm.at[1, 1], a_ref.at[1]),
                 (d_hbm.at[0, 0], d_ref.at[0]),
                 (d_hbm.at[0, 1], d_ref.at[1]),
+                (a_hbm.at[0], a_first),
+                (c_hbm.at[0], c_first),
+                (g_hbm.at[0], g_first),
             )
         )
     ]
@@ -125,16 +129,22 @@
         chunk = mod4(x + shift)
         for part in range(2):
             piece[:, pl.ds(1152 + part * 256, 256)] = d_ref[part, :, at(chunk, 256)]
-
-
-def couplings_kernel(s_ref, a_ref, c_ref, a_even, c_even):
-    first_row = (s_ref[0] * 4 + s_ref[1]) * 64
-    before, own, odd = s_ref[2], s_ref[3], s_ref[4]
+    copies[7].wait()
+    copies[8].wait()
     for chunk in range(4):
         cols = pl.ds(chunk * 256, 256)
         for part in range(2):
-            a_even[part, :, cols] = masked(a_ref[part, :, cols], first_row, own, chunk, before)
-            c_even[part, :, cols] = masked(c_ref[part, :, cols], first_row, own, chunk, odd)
+            a_even[part, :, cols] = masked(a_first[part, :, cols], first_row, own, chunk, before)
+            c_even[part, :, cols] = masked(c_first[part, :, cols], first_row, own, chunk, odd)
+    copies[9].wait()
+    for shift, piece in enumerate((g0, g1, g2, g3)):
+        for part in range(2):
+            piece[part] = g_first[part, :, at(mod4(y + shift), 256)]
+
+
+def columns_kernel(s_ref, g0, g1, g2, g3, out):
+    for shift, piece in enumerate((g0, g1, g2, g3)):
+        out[mod4(s_ref[0] - shift)] = piece[...]
 
 
 def assemble_kernel(s_ref, piece0, piece1, piece2, piece3, panel, panel_a, diagonal):
@@ -193,13 +203,14 @@
     put_pair(out, *wide_product(s_ref[0], g_rows, (panel0, panel1, panel2, panel3)))
 
 
-def even_kernel(s_ref, ca0, ca1, ca2, ca3, panel0, panel1, panel2, panel3, source,
+def even_kernel(s_ref, ca, panel0, panel1, panel2, panel3, source,
                 ship, upper_new, source_part, a_rows, c_rows):
-    y, x = s_ref[0], s_ref[1]
+    y = s_ref[0]
     panels = (panel0, panel1, panel2, panel3)
-    blocks = (ca0, ca1, ca2, ca3)
-    stack_rows(x, [b.at[1] for b in blocks], a_rows)
-    stack_rows(x, [b.at[0] for b in blocks], c_rows)
+    for index in range(4):
+        rows = pl.ds(index * 128, 128)
+        c_rows[rows, :] = ca[index, 0].reshape(128, 1024)
+        a_rows[rows, :] = ca[index, 1].reshape(128, 1024)
     ship[:, pl.ds(512, 128)] = small_product(y, a_rows, panels).astype(BF)
     put_pair(ship, *wide_product(y, a_rows, panels))
     own = pltpu.roll(source[:, pl.ds(512, 128)].astype(F32), 64, 1)
@@ -209,47 +220,19 @@
     put_pair(upper_new, -real, -imag)
 
 
-def source_kernel(s_ref, source_part, shipped, source_new):
-    source_new[...] = packed(
-        source_part[...] - shipped[:, pl.ds(512, 128)].astype(F32)
-    ).astype(BF)
-
-
-def diagonal_kernel(s_ref, c_rows, panel0, panel1, panel2, panel3, diagonal, shipped, out):
+def diagonal_kernel(s_ref, c_rows, a_rows, panel0, panel1, panel2, panel3, diagonal, shipped,
+                    out, lower):
     real, imag = wide_product(s_ref[0], c_rows, (panel0, panel1, panel2, panel3))
     real = diagonal[:, pl.ds(0, 256)].astype(F32) - real - shipped[:, pl.ds(0, 256)].astype(F32)
     imag = diagonal[:, pl.ds(256, 256)].astype(F32) - imag - shipped[:, pl.ds(256, 256)].astype(F32)
     put_pair(out, real, imag)
-
-
-def lower_kernel(s_ref, a_rows, panel0, panel1, panel2, panel3, out):
     real, imag = wide_product(s_ref[0], a_rows, (panel0, panel1, panel2, panel3))
-    put_pair(out, -real, -imag)
+    put_pair(lower, -real, -imag)
 
 
 def pair_kernel(s_ref, lower, upper, out):
     out[:, pl.ds(0, 512)] = lower[...]
     out[:, pl.ds(512, 512)] = upper[...]
-
-
-def whole_inverse(y, g_ref, pieces, vector):
-    for place, piece in enumerate(pieces):
-        for index, half in enumerate(halves(piece[...].astype(F32))):
-            rows = pl.ds(pl.multiple_of(mod4(y + place) * 256 + index * 128, 128), 128)
-            vector[rows, :] = half.astype(BF)
-    right = vector[...]
-    for block in range(4):
-        left = g_ref[pl.ds(block * 4, 4)].reshape(512, 1024)
-        total = jnp.dot(left, right, preferred_element_type=F32).reshape(4, 2, 64, 128)
-        yield block, combine_small(
-            total[:, 0].reshape(256, 128), total[:, 1].reshape(256, 128)
-        )
-
-
-def solve_kernel(s_ref, g_ref, piece0, piece1, piece2, piece3, out, vector):
-    pieces = (piece0, piece1, piece2, piece3)
-    for block, value in whole_inverse(s_ref[0], g_ref, pieces, vector):
-        out[pl.ds(block * 256, 256), :] = value.astype(BF)
 
 
 def block_product(block, right):
@@ -258,35 +241,55 @@
     return real, imag
 
 
-def residue_of(x, blocks, source, solved):
+def put_partial(g_ref, right, own, send, whole):
+    for index in range(4):
+        total = jnp.dot(g_ref[index].reshape(512, 256), right, preferred_element_type=F32)
+        parts = total.reshape(4, 2, 64, 128)
+        value = combine_small(parts[:, 0].reshape(256, 128), parts[:, 1].reshape(256, 128))
+        value = value.reshape(4, 64, 128)
+        for group in range(4):
+            whole[pl.ds(group * 256 + index * 64, 64), :] = value[group]
+    total = packed(whole[...])
+    own[...] = total
+    send[...] = total.astype(BF)
+
+
+def source_kernel(s_ref, g_ref, source_part, shipped, source_new, own, send, whole):
+    source = (source_part[...] - shipped[:, pl.ds(512, 128)].astype(F32)).astype(BF)
+    source_new[...] = source
+    put_partial(g_ref, source, own, send, whole)
+
+
+def summed(own, got):
+    total = own[...]
+    for other in got:
+        total = total + other[...].astype(F32)
+    return total
+
+
+def turn_kernel(s_ref, own, got1, got2, got3, *refs, first):
+    solved = None if first else refs[0]
+    blocks, refs = refs[:4] if first else refs[1:5], refs[4:] if first else refs[5:]
+    source, g_ref, out, own_new, send, vector, whole = refs
+    x = s_ref[1]
+    total = summed(own, (got1, got2, got3))
+    if not first:
+        total = solved[...].astype(F32) + total
+    out[...] = total.astype(BF)
+    low, high = halves(out[...].astype(F32))
+    vector[pl.ds(0, 512), :] = low.astype(BF)
+    vector[pl.ds(512, 512), :] = high.astype(BF)
     real_rows = imag_rows = None
     for shift, block in enumerate(blocks):
-        real, imag = block_product(block, solved[at(mod4(x - shift), 256), :])
+        real, imag = block_product(block, vector[at(mod4(x - shift), 256), :])
         real_rows = real if real_rows is None else real_rows + real
         imag_rows = imag if imag_rows is None else imag_rows + imag
-    value = packed(combine_small(real_rows, imag_rows))
-    return (source[...].astype(F32) - value).astype(BF)
-
-
-def residue_kernel(s_ref, block0, block1, block2, block3, source, solved, out):
-    out[...] = residue_of(s_ref[1], (block0, block1, block2, block3), source, solved)
-
-
-def turn_kernel(s_ref, g_ref, piece0, piece1, piece2, piece3, solved,
-                block0, block1, block2, block3, source, out, residue, vector):
-    pieces = (piece0, piece1, piece2, piece3)
-    for block, value in whole_inverse(s_ref[0], g_ref, pieces, vector):
-        rows = pl.ds(block * 256, 256)
-        out[rows, :] = (solved[rows, :].astype(F32) + value).astype(BF)
-    residue[...] = residue_of(s_ref[1], (block0, block1, block2, block3), source, out)
-
-
-def last_kernel(s_ref, g_ref, piece0, piece1, piece2, piece3, solved, out, ship, vector):
-    pieces = (piece0, piece1, piece2, piece3)
-    for block, value in whole_inverse(s_ref[0], g_ref, pieces, vector):
-        rows = pl.ds(block * 256, 256)
-        out[rows, :] = (solved[rows, :].astype(F32) + value).astype(BF)
-    ship[...] = packed(out[...].astype(F32)).astype(BF)
+    residue = (source[...].astype(F32) - combine_small(real_rows, imag_rows)).astype(BF)
+    put_partial(g_ref, residue, own_new, send, whole)
+
+
+def last_kernel(s_ref, own, got1, got2, got3, solved, out):
+    out[...] = (solved[...].astype(F32) + summed(own, (got1, got2, got3))).astype(BF)
 
 
 def diagonal_rows_kernel(s_ref, block0, block1, block2, block3, rows_out):
@@ -325,14 +328,10 @@
 
 def couple_kernel(s_ref, pairs, source, solved, below, above, out0, out1, out2, out3, held):
     y, x = s_ref[0], s_ref[1]
-    combined = -coupled(pairs, 0, below) - coupled(pairs, 512, above)
-    for index, half in enumerate(halves(source[...].astype(F32))):
-        rows = pl.ds(index * 128, 128)
-        moved = pltpu.roll(
-            solved[pl.ds(pl.multiple_of(y * 256 + index * 128, 128), 128), :].astype(F32), 64, 1
-        )
-        total = half + combined[index * 128 : index * 128 + 128]
-        held[rows, :] = jnp.where(lanes_of(128) < 64, total, moved)
+    combined = source[...].astype(F32) - coupled(pairs, 0, below) - coupled(pairs, 512, above)
+    rows = pl.ds(pl.multiple_of(lax.rem(y, 2) * 256, 256), 256)
+    moved = pltpu.roll(solved[rows, :].astype(F32), jnp.where(y < 2, 64, 0), 1)
+    held[...] = jnp.where(lanes_of(256) < 64, combined, moved)
     for shift, out in enumerate((out0, out1, out2, out3)):
         out[...] = held[at(mod4(x + shift), 64), :]
 
@@ -386,38 +385,39 @@
     window = lax.dynamic_slice_in_dim(jnp.concatenate([zero, orbitals, zero]), 2 * cut, 4)
     scalars = jnp.concatenate([jnp.stack([place // 4, place % 4]).astype(jnp.int32), window])
     turns = (1, 2, 3)
+    after = lax.optimization_barrier
     wide_flops = 2 * 512 * 1024 * 512
-    solve_flops = 2 * 2048 * 1024 * 128
-    vector = pltpu.VMEM((1024, 128), BF)
-
-    pieces = call(
+    solve_flops = 2 * 2048 * 256 * 128
+
+    *pieces, a_even, c_even, g0, g1, g2, g3 = call(
         prepare_kernel,
-        [shape((64, 1664))] * 4,
+        [shape((64, 1664))] * 4 + [shape((2, 64, 1024))] * 2 + [shape((2, 64, 256))] * 4,
         0,
-        scalars, diagonal_blocks, lower_blocks, upper_blocks, injection,
-        hbm=4,
+        scalars, diagonal_blocks, diagonal_inverses, lower_blocks, upper_blocks, injection,
+        hbm=5, mib=60,
         scratch=[pltpu.VMEM((2, 64, 1024), BF)] * 3
-        + [pltpu.VMEM((2, 2, 64, 128), BF), pltpu.SemaphoreType.DMA((7,))],
-    )
-    inverse_even = lax.all_gather(diagonal_inverses[0], "row")
+        + [pltpu.VMEM((2, 2, 64, 128), BF)]
+        + [pltpu.VMEM((2, 64, 1024), BF)] * 3
+        + [pltpu.SemaphoreType.DMA((10,))],
+    )
     pieces = [pieces[0]] + [moved_x(pieces[by], by) for by in turns]
-    a_even, c_even = call(
-        couplings_kernel,
-        [shape((2, 64, 1024))] * 2,
-        0,
-        scalars, lower_blocks[0], upper_blocks[0],
-    )
-    couplings = jnp.stack([c_even, along_cuts(a_even, -1)])
-    g_odd = diagonal_inverses[1]
-    g_blocks = [g_odd] + [moved_x(g_odd, by) for by in turns]
+    a_next = along_cuts(a_even, -1)
+    a_next, g_odd, g1, g2, g3, *pieces = after(
+        (a_next, diagonal_inverses[1], g1, g2, g3, *pieces)
+    )
+    couplings = gathered_x(jnp.stack([c_even, a_next]))
+    g_pieces = [g0] + [moved_y(piece, by) for by, piece in zip(turns, (g1, g2, g3))]
     panel, panel_a, diagonal = call(
         assemble_kernel,
         [shape((256, 640)), shape((256, 512)), shape((256, 512))],
         0, scalars, *pieces,
     )
     panels = gathered_y(panel)
+    g_blocks = [g_odd] + [moved_x(g_odd, by) for by in turns]
+    panel_a, *panels_and = after((panel_a, *panels, *g_pieces))
+    panels, g_pieces = panels_and[:4], panels_and[4:]
+    (g_columns,) = call(columns_kernel, [shape((4, 2, 64, 256))], 0, scalars, *g_pieces)
     panels_a = gathered_y(panel_a)
-    ca_blocks = [couplings] + [moved_x(couplings, by) for by in turns]
     first, g_rows = call(
         odd_kernel, [shape((256, 640)), shape((512, 1024))], wide_flops,
         scalars, *g_blocks, *panels, scratch=[pltpu.VMEM((512, 1024), BF)],
@@ -432,41 +432,44 @@
         [shape((256, 640)), shape((256, 512)), shape((256, 128), F32), shape((512, 1024)),
          shape((512, 1024))],
         2 * wide_flops,
-        scalars, *ca_blocks, *firsts, panel,
+        scalars, couplings, *firsts, panel,
     )
     shipped = along_cuts(ship, 1)
-    (source,) = call(source_kernel, [shape((128, 128))], 0, scalars, source_part, shipped)
-    sources = gathered_y(source)
-    (diagonal_new,) = call(
-        diagonal_kernel, [shape((256, 512))], wide_flops,
-        scalars, c_rows, *seconds, diagonal, shipped,
-    )
+    g_columns = gathered_x(g_columns)
+    shipped, *seconds = after((shipped, *seconds))
+    diagonal_new, ship_lower = call(
+        diagonal_kernel, [shape((256, 512))] * 2, 2 * wide_flops,
+        scalars, c_rows, a_rows, *seconds, diagonal, shipped,
+    )
+    source_part, diagonal_new = after((source_part, diagonal_new))
     diagonals = [diagonal_new] + [moved_x(diagonal_new, by) for by in turns]
-    (ship_lower,) = call(
-        lower_kernel, [shape((256, 512))], wide_flops, scalars, a_rows, *seconds
+    packed_shapes = [shape((512, 128), F32), shape((512, 128))]
+    whole = pltpu.VMEM((1024, 128), F32)
+    vector = pltpu.VMEM((1024, 128), BF)
+    source, own, send = call(
+        source_kernel, [shape((256, 128))] + packed_shapes, solve_flops,
+        scalars, g_columns, source_part, shipped, scratch=[whole],
     )
     lower_new = along_cuts(ship_lower, 1)
+    got = gathered_y(send)[1:]
+    lower_new, *both = after((lower_new, *diagonals, *got))
+    diagonals, got = both[:4], both[4:]
     (pair,) = call(pair_kernel, [shape((256, 1024))], 0, scalars, lower_new, upper_new)
     pairs = gathered_x(pair)
+    solved = ()
+    for turn in range(REFINE):
+        *solved, own, send = call(
+            functools.partial(turn_kernel, first=turn == 0),
+            [shape((512, 128))] + packed_shapes, 2 * solve_flops,
+            scalars, own, *got, *solved, *diagonals, source, g_columns,
+            scratch=[vector, whole],
+        )
+        got = gathered_y(send)[1:]
     (solved,) = call(
-        solve_kernel, [shape((1024, 128))], solve_flops,
-        scalars, inverse_even, *sources, scratch=[vector],
-    )
-    (residue,) = call(
-        residue_kernel, [shape((128, 128))], solve_flops // 4,
-        scalars, *diagonals, source, solved,
-    )
-    for _ in range(REFINE - 1):
-        solved, residue = call(
-            turn_kernel, [shape((1024, 128)), shape((128, 128))], solve_flops,
-            scalars, inverse_even, *gathered_y(residue), solved, *diagonals, source,
-            scratch=[vector],
-        )
-    solved, ship_solved = call(
-        last_kernel, [shape((1024, 128)), shape((512, 128))], solve_flops,
-        scalars, inverse_even, *gathered_y(residue), solved, scratch=[vector],
-    )
-    below, above = along_cuts(ship_solved, 1), along_cuts(ship_solved, -1)
+        last_kernel, [shape((512, 128))], 0,
+        scalars, own, *got, *solved,
+    )
+    below, above = along_cuts(solved, 1), along_cuts(solved, -1)
     (diagonal_rows,) = call(
         diagonal_rows_kernel, [shape((2, 64, 1024))], 0, scalars, *diagonals
     )

time: 216 us -> 212 us (0.981)
  waiting for transfers between devices: 102 us -> 99.1 us
  starting transfers between devices: 62 us -> 59.5 us
  other arithmetic: 0.86 us -> 3.14 us
    ppermute x5, waiting for transfers between devices: 12.8 us -> 5.57 us  [along_cuts(): return lax.ppermute(block, 'cuts', pairs)]
    ppermute x21 -> x24, waiting for transfers between devices: 60.3 us -> 67 us  [moved_y(): return lax.ppermute(block, 'row', pairs)]
    ppermute x5, starting transfers between devices: 24 us -> 18.4 us  [along_cuts(): return lax.ppermute(block, 'cuts', pairs)]
    ppermute x15 -> x12, starting transfers between devices: 12.6 us -> 16.5 us  [moved_x(): return lax.ppermute(block, 'row', pairs)]
    unnamed x16 -> x40, local copies, waits for them, and re-layouts: 7.77 us -> 10.3 us
    ppermute x15 -> x12, waiting for transfers between devices: 28.8 us -> 26.5 us  [moved_x(): return lax.ppermute(block, 'row', pairs)]
    pallas_call x18 -> x16, Pallas kernels: 26.3 us -> 24.9 us  [call(): pl.pallas_call(kernel, out_shape=tuple(out_shapes), in_specs=[SMEM] + [an...]
    ppermute x21 -> x24, starting transfers between devices: 25.2 us -> 24.5 us  [moved_y(): return lax.ppermute(block, 'row', pairs)]
  transfers between devices with their start and end apart: 43 -> 44, of which waited for: 24 -> 23; matrix products, arithmetic and copies ran while one was open for 0% -> 0% of each run, Pallas kernels for 11% -> 8%
where the time goes in v3:
time: 212 us; the launch traced here: 211 us
  waiting for transfers between devices  99.1 us (47%)
  starting transfers between devices  59.5 us (28%)
  Pallas kernels  24.9 us (12%)
  between operations  14.1 us (7%)
  local copies, waits for them, and re-layouts  10.4 us (5%)
  other arithmetic  3.14 us (1%)
    ppermute x24, waiting for transfers between devices, moved_y(): return lax.ppermute(block, 'row', pairs)  67 us
    ppermute x12, waiting for transfers between devices, moved_x(): return lax.ppermute(block, 'row', pairs)  26.5 us
    pallas_call x16, Pallas kernels, call(): pl.pallas_call(kernel, out_shape=tuple(out_shapes), in_specs=[SMEM] + [an...  24.9 us
    ppermute x24, starting transfers between devices, moved_y(): return lax.ppermute(block, 'row', pairs)  24.5 us
    ppermute x5, starting transfers between devices, along_cuts(): return lax.ppermute(block, 'cuts', pairs)  18.4 us
    ppermute x12, starting transfers between devices, moved_x(): return lax.ppermute(block, 'row', pairs)  16.5 us
    unnamed x40, local copies, waits for them, and re-layouts  10.3 us
    ppermute x5, waiting for transfers between devices, along_cuts(): return lax.ppermute(block, 'cuts', pairs)  5.57 us
  transfers between devices with their start and end apart: 44, of which 23 were waited for; matrix products, arithmetic and copies ran while one was open for 0% of the time, Pallas kernels for 8%

profile of v3, /device:TPU:97, one launch (start us, length us, event | category | flops | bytes accessed | tf_op | source)
XLA Modules:
  0.0 211.1 jit_solution(2558661598492588347)
XLA Ops:
  8.7 3.5 %shard_map.101 = (bf16[64,1664]{1,0:T(8,128)(2,1)}, bf16[64,1664]{1,0:T(8,128)(2,1)}, bf16[64,1664]{1,0:T(8,128)(2,1)}, bf16[64,1664]{1,0:T(8,128)(2,1)}, bf16[2...) custom-call(s32[6]{0:T(128)} %pad_add_fusion.1.s_ref, ...), custom_call_target="tpu_custom_call" | custom-call | bytes 3801112 | tf_op jit(solution)/shard_map/pallas_call | solution.py:22
  12.3 2.7 %collective-permute-start = (bf16[2,64,1024]{2,1,0:T(8,128)(2,1)}, bf16[2,64,1024]{2,1,0:T(8,128)(2,1)S(1)}, u32[]{:S(2)}, u32[]{:S(2)}) collective-permute-start(bf16[2,64,1024]{2,1,0:T(8,128)(2,1)} %get-tuple-element.78), channel_id=1, source_target_pairs={{16,0},{32,16},{48,32},{64,48},{80,64},{96,80},{112,96},{128,112},... | collective-permute-start | bytes 786440 | tf_op jit(solution)/shard_map/ppermute | solution.py:378
  16.3 2.5 %collective-permute-start.2 = (bf16[64,1664]{1,0:T(8,128)(2,1)}, bf16[64,1664]{1,0:T(8,128)(2,1)S(1)}, u32[]{:S(2)}, u32[]{:S(2)}) collective-permute-start(bf16[64,1664]{1,0:T(8,128)(2,1)} %get-tuple-element.84), channel_id=1, source_target_pairs={{0,2},{1,3},{2,0},{3,1},{4,6},{5,7},{6,4},{7,5},{8,10},{9,11},{10,... | collective-permute-start | bytes 638984 | tf_op jit(solution)/shard_map/ppermute | solution.py:358
  19.9 3.5 %collective-permute-done.1.piece1 = bf16[64,1664]{1,0:T(8,128)(2,1)S(1)} collective-permute-done((bf16[64,1664]{1,0:T(8,128)(2,1)}, bf16[64,1664]{1,0:T(8,128)(2,1)S(1)}, u32[]{:S(2)}, u32[]{:S(2)}) %collective-permute-start.1) | collective-permute-done | bytes 213024 | tf_op jit(solution)/shard_map/ppermute | solution.py:358
  23.4 5.5 %collective-permute-done.2.piece2 = bf16[64,1664]{1,0:T(8,128)(2,1)S(1)} collective-permute-done((bf16[64,1664]{1,0:T(8,128)(2,1)}, bf16[64,1664]{1,0:T(8,128)(2,1)S(1)}, u32[]{:S(2)}, u32[]{:S(2)}) %collective-permute-start.2) | collective-permute-done | bytes 213024 | tf_op jit(solution)/shard_map/ppermute | solution.py:358
  32.1 2.7 %collective-permute-start.7 = (bf16[256,640]{1,0:T(8,128)(2,1)S(1)}, bf16[256,640]{1,0:T(8,128)(2,1)S(1)}, u32[]{:S(2)}, u32[]{:S(2)}) collective-permute-start(bf16[256,640]{1,0:T(8,128)(2,1)S(1)} %get-tuple-element.98.panel0.source), channel_id=1, source_target_pairs={{0,12},{1,13},{2,14},{3,15},{4,0},{5,1},{6,2},{7,3},{8,4},{9,5},{1... | collective-permute-start | bytes 983048 | tf_op jit(solution)/shard_map/ppermute | solution.py:363
  39.1 16.2 %collective-permute-done.10.g1 = bf16[2,64,256]{2,1,0:T(8,128)(2,1)S(1)} collective-permute-done((bf16[2,64,256]{2,1,0:T(8,128)(2,1)S(1)}, bf16[2,64,256]{2,1,0:T(8,128)(2,1)S(1)}, u32[]{:S(2)}, u32[]{:S(2)}) %collective-permute-start.10) | collective-permute-done | bytes 65568 | tf_op jit(solution)/shard_map/ppermute | solution.py:363
  55.3 3.5 %collective-permute-done.12.g3 = bf16[2,64,256]{2,1,0:T(8,128)(2,1)S(1)} collective-permute-done((bf16[2,64,256]{2,1,0:T(8,128)(2,1)S(1)}, bf16[2,64,256]{2,1,0:T(8,128)(2,1)S(1)}, u32[]{:S(2)}, u32[]{:S(2)}) %collective-permute-start.12) | collective-permute-done | bytes 65568 | tf_op jit(solution)/shard_map/ppermute | solution.py:363
  60.8 2.9 %collective-permute-start.5 = (bf16[2,64,1024]{2,1,0:T(8,128)(2,1)S(1)}, bf16[2,64,1024]{2,1,0:T(8,128)(2,1)S(1)}, u32[]{:S(2)}, u32[]{:S(2)}) collective-permute-start(bf16[2,64,1024]{2,1,0:T(8,128)(2,1)S(1)} %slice_bitcast_fusion.g0), channel_id=1, source_target_pairs={{0,2},{1,3},{2,0},{3,1},{4,6},{5,7},{6,4},{7,5},{8,10},{9,11},{10,... | collective-permute-start | bytes 786440 | tf_op jit(solution)/shard_map/ppermute | solution.py:358
  64.2 6.6 %collective-permute-done.4.g1 = bf16[2,64,1024]{2,1,0:T(8,128)(2,1)S(1)} collective-permute-done((bf16[2,64,1024]{2,1,0:T(8,128)(2,1)S(1)}, bf16[2,64,1024]{2,1,0:T(8,128)(2,1)S(1)}, u32[]{:S(2)}, u32[]{:S(2)}) %collective-permute-start.4) | collective-permute-done | bytes 262176 | tf_op jit(solution)/shard_map/ppermute | solution.py:358
  70.9 5.9 %collective-permute-done.5.g2 = bf16[2,64,1024]{2,1,0:T(8,128)(2,1)S(1)} collective-permute-done((bf16[2,64,1024]{2,1,0:T(8,128)(2,1)S(1)}, bf16[2,64,1024]{2,1,0:T(8,128)(2,1)S(1)}, u32[]{:S(2)}, u32[]{:S(2)}) %collective-permute-start.5) | collective-permute-done | bytes 262176 | tf_op jit(solution)/shard_map/ppermute | solution.py:358
  78.5 2.5 %collective-permute-start.13 = (bf16[256,640]{1,0:T(8,128)(2,1)S(1)}, bf16[256,640]{1,0:T(8,128)(2,1)S(1)}, u32[]{:S(2)}, u32[]{:S(2)}) collective-permute-start(bf16[256,640]{1,0:T(8,128)(2,1)S(1)} %get-tuple-element.102.panel0), channel_id=1, source_target_pairs={{0,12},{1,13},{2,14},{3,15},{4,0},{5,1},{6,2},{7,3},{8,4},{9,5},{1... | collective-permute-start | bytes 983048 | tf_op jit(solution)/shard_map/ppermute | solution.py:363
  82.2 2.0 collective-permute-start.17
  85.4 2.1 %collective-permute-done.13.panel1 = bf16[256,640]{1,0:T(8,128)(2,1)S(1)} collective-permute-done((bf16[256,640]{1,0:T(8,128)(2,1)S(1)}, bf16[256,640]{1,0:T(8,128)(2,1)S(1)}, u32[]{:S(2)}, u32[]{:S(2)}) %collective-permute-start.13) | collective-permute-done | bytes 327712 | tf_op jit(solution)/shard_map/ppermute | solution.py:363
  91.1 9.8 %collective-permute-done.15.panel3 = bf16[256,640]{1,0:T(8,128)(2,1)S(1)} collective-permute-done((bf16[256,640]{1,0:T(8,128)(2,1)S(1)}, bf16[256,640]{1,0:T(8,128)(2,1)S(1)}, u32[]{:S(2)}, u32[]{:S(2)}) %collective-permute-start.15) | collective-permute-done | bytes 327712 | tf_op jit(solution)/shard_map/ppermute | solution.py:363
  106.2 2.4 %shard_map.104 = (bf16[256,640]{1,0:T(8,128)(2,1)S(1)}, bf16[256,512]{1,0:T(8,128)(2,1)S(1)}, f32[256,128]{1,0:T(8,128)S(1)}, bf16[512,1024]{1,0:T(8,128)(2,1)S(1)}, bf16[512,1024]{1,0:T(8,128)(2,1)S(1)}) custom-call(s32[6]{0:T(128)S(1)} %copy-done.5, bf16[4,2,2,64,1024]{4,3,2,1,0:T(8,128)(2,1)S(1)} %bitcast.19, ...), custom_call_target="tpu_custom_call" | custom-call | flops 1073741824 | bytes 6553624 | tf_op jit(solution)/shard_map/pallas_call | solution.py:22
  108.6 5.0 %collective-permute-start.16 = (bf16[256,640]{1,0:T(8,128)(2,1)S(1)}, bf16[256,640]{1,0:T(8,128)(2,1)S(1)}, u32[]{:S(2)}, u32[]{:S(2)}) collective-permute-start(bf16[256,640]{1,0:T(8,128)(2,1)S(1)} %get-tuple-element.105), channel_id=1, source_target_pairs={{0,16},{16,32},{32,48},{48,64},{64,80},{80,96},{96,112},{112,128},... | collective-permute-start | bytes 983048 | tf_op jit(solution)/shard_map/ppermute | solution.py:378
  118.2 5.3 %collective-permute-done.20.panel1 = bf16[256,512]{1,0:T(8,128)(2,1)S(1)} collective-permute-done((bf16[256,512]{1,0:T(8,128)(2,1)S(1)}, bf16[256,512]{1,0:T(8,128)(2,1)S(1)}, u32[]{:S(2)}, u32[]{:S(2)}) %collective-permute-start.20) | collective-permute-done | bytes 262176 | tf_op jit(solution)/shard_map/ppermute | solution.py:363
  123.4 2.1 collective-permute-done.21.panel2
  125.5 4.1 %collective-permute-done.22.panel3 = bf16[256,512]{1,0:T(8,128)(2,1)S(1)} collective-permute-done((bf16[256,512]{1,0:T(8,128)(2,1)S(1)}, bf16[256,512]{1,0:T(8,128)(2,1)S(1)}, u32[]{:S(2)}, u32[]{:S(2)}) %collective-permute-start.22) | collective-permute-done | bytes 262176 | tf_op jit(solution)/shard_map/ppermute | solution.py:363
  135.3 5.3 %collective-permute-start.23 = (bf16[256,512]{1,0:T(8,128)(2,1)S(1)}, bf16[256,512]{1,0:T(8,128)(2,1)S(1)}, u32[]{:S(2)}, u32[]{:S(2)}) collective-permute-start(bf16[256,512]{1,0:T(8,128)(2,1)S(1)} %get-tuple-element.114), channel_id=1, source_target_pairs={{0,16},{16,32},{32,48},{48,64},{64,80},{80,96},{96,112},{112,128},... | collective-permute-start | bytes 786440 | tf_op jit(solution)/shard_map/ppermute | solution.py:378
  144.4 4.9 %collective-permute-done.29.got3 = bf16[512,128]{1,0:T(8,128)(2,1)S(1)} collective-permute-done((bf16[512,128]{1,0:T(8,128)(2,1)S(1)}, bf16[512,128]{1,0:T(8,128)(2,1)S(1)}, u32[]{:S(2)}, u32[]{:S(2)}) %collective-permute-start.29) | collective-permute-done | bytes 131104 | tf_op jit(solution)/shard_map/ppermute | solution.py:363
  149.3 4.0 %collective-permute-done.24.block1.refs_1_.refs_2_ = bf16[256,512]{1,0:T(8,128)(2,1)S(1)} collective-permute-done((bf16[256,512]{1,0:T(8,128)(2,1)S(1)}, bf16[256,512]{1,0:T(8,128)(2,1)S(1)}, u32[]{:S(2)}, u32[]{:S(2)}) %collective-permute-start.24) | collective-permute-done | bytes 262176 | tf_op jit(solution)/shard_map/ppermute | solution.py:358
  157.4 2.8 %collective-permute-start.30 = (bf16[512,128]{1,0:T(8,128)(2,1)S(1)}, bf16[512,128]{1,0:T(8,128)(2,1)S(1)}, u32[]{:S(2)}, u32[]{:S(2)}) collective-permute-start(bf16[512,128]{1,0:T(8,128)(2,1)S(1)} %get-tuple-element.138), channel_id=1, source_target_pairs={{0,12},{1,13},{2,14},{3,15},{4,0},{5,1},{6,2},{7,3},{8,4},{9,5},{1... | collective-permute-start | bytes 393224 | tf_op jit(solution)/shard_map/ppermute | solution.py:363
  160.9 5.4 %collective-permute-done.30.got1 = bf16[512,128]{1,0:T(8,128)(2,1)S(1)} collective-permute-done((bf16[512,128]{1,0:T(8,128)(2,1)S(1)}, bf16[512,128]{1,0:T(8,128)(2,1)S(1)}, u32[]{:S(2)}, u32[]{:S(2)}) %collective-permute-start.30) | collective-permute-done | bytes 131104 | tf_op jit(solution)/shard_map/ppermute | solution.py:363
  167.0 2.5 %collective-permute-done.32.got3 = bf16[512,128]{1,0:T(8,128)(2,1)S(1)} collective-permute-done((bf16[512,128]{1,0:T(8,128)(2,1)S(1)}, bf16[512,128]{1,0:T(8,128)(2,1)S(1)}, u32[]{:S(2)}, u32[]{:S(2)}) %collective-permute-start.32) | collective-permute-done | bytes 131104 | tf_op jit(solution)/shard_map/ppermute | solution.py:363
  172.9 3.0 %collective-permute-done.33.got1 = bf16[512,128]{1,0:T(8,128)(2,1)S(1)} collective-permute-done((bf16[512,128]{1,0:T(8,128)(2,1)S(1)}, bf16[512,128]{1,0:T(8,128)(2,1)S(1)}, u32[]{:S(2)}, u32[]{:S(2)}) %collective-permute-start.33) | collective-permute-done | bytes 131104 | tf_op jit(solution)/shard_map/ppermute | solution.py:363
  177.4 4.4 %collective-permute-done.35.got3 = bf16[512,128]{1,0:T(8,128)(2,1)S(1)} collective-permute-done((bf16[512,128]{1,0:T(8,128)(2,1)S(1)}, bf16[512,128]{1,0:T(8,128)(2,1)S(1)}, u32[]{:S(2)}, u32[]{:S(2)}) %collective-permute-start.35) | collective-permute-done | bytes 131104 | tf_op jit(solution)/shard_map/ppermute | solution.py:363
  182.4 3.4 %collective-permute-start.36 = (bf16[512,128]{1,0:T(8,128)(2,1)S(1)}, bf16[512,128]{1,0:T(8,128)(2,1)S(1)}, u32[]{:S(2)}, u32[]{:S(2)}) collective-permute-start(bf16[512,128]{1,0:T(8,128)(2,1)S(1)} %shard_map.114.solved), channel_id=1, source_target_pairs={{0,16},{16,32},{32,48},{48,64},{64,80},{80,96},{96,112},{112,128},... | collective-permute-start | bytes 393224 | tf_op jit(solution)/shard_map/ppermute | solution.py:378
  185.8 1.9 collective-permute-start.37
  187.7 5.6 %collective-permute-done.37.above = bf16[512,128]{1,0:T(8,128)(2,1)S(1)} collective-permute-done((bf16[512,128]{1,0:T(8,128)(2,1)S(1)}, bf16[512,128]{1,0:T(8,128)(2,1)S(1)}, u32[]{:S(2)}, u32[]{:S(2)}) %collective-permute-start.37) | collective-permute-done | bytes 131104 | tf_op jit(solution)/shard_map/ppermute | solution.py:378
  197.4 3.0 %collective-permute-start.39 = (f32[64,128]{1,0:T(8,128)S(1)}, f32[64,128]{1,0:T(8,128)S(1)}, u32[]{:S(2)}, u32[]{:S(2)}) collective-permute-start(f32[64,128]{1,0:T(8,128)S(1)} %get-tuple-element.145), channel_id=1, source_target_pairs={{0,2},{1,3},{2,0},{3,1},{4,6},{5,7},{6,4},{7,5},{8,10},{9,11},{10,... | collective-permute-start | bytes 98312 | tf_op jit(solution)/shard_map/ppermute | solution.py:358
  (120 shorter events, 60.1 us)
Async XLA Ops:
  7.2 94.5 %all-gather.7.cloned.1.call-start = ((), (), s32[]{:S(2)}) async-start(), calls=%async_computation | async-start | bytes 2621440 | tf_op jit(solution)/shard_map/all_gather | solution.py:372
  12.3 16.6 %collective-permute-start = (bf16[2,64,1024]{2,1,0:T(8,128)(2,1)}, bf16[2,64,1024]{2,1,0:T(8,128)(2,1)S(1)}, u32[]{:S(2)}, u32[]{:S(2)}) collective-permute-start(bf16[2,64,1024]{2,1,0:T(8,128)(2,1)} %get-tuple-element.78), channel_id=1, source_target_pairs={{16,0},{32,16},{48,32},{64,48},{80,64},{96,80},{112,96},{128,112},... | collective-permute-start | bytes 786440 | tf_op jit(solution)/shard_map/ppermute | solution.py:378
  16.3 12.6 %collective-permute-start.2 = (bf16[64,1664]{1,0:T(8,128)(2,1)}, bf16[64,1664]{1,0:T(8,128)(2,1)S(1)}, u32[]{:S(2)}, u32[]{:S(2)}) collective-permute-start(bf16[64,1664]{1,0:T(8,128)(2,1)} %get-tuple-element.84), channel_id=1, source_target_pairs={{0,2},{1,3},{2,0},{3,1},{4,6},{5,7},{6,4},{7,5},{8,10},{9,11},{10,... | collective-permute-start | bytes 638984 | tf_op jit(solution)/shard_map/ppermute | solution.py:358
  18.7 10.2 %collective-permute-start.3 = (bf16[64,1664]{1,0:T(8,128)(2,1)}, bf16[64,1664]{1,0:T(8,128)(2,1)S(1)}, u32[]{:S(2)}, u32[]{:S(2)}) collective-permute-start(bf16[64,1664]{1,0:T(8,128)(2,1)} %get-tuple-element.85), channel_id=1, source_target_pairs={{0,3},{1,0},{2,1},{3,2},{4,7},{5,4},{6,5},{7,6},{8,11},{9,8},{10,9... | collective-permute-start | bytes 638984 | tf_op jit(solution)/shard_map/ppermute | solution.py:358
  30.7 100.6 %all-gather.9.cloned.1.call-start = ((), (), s32[]{:S(2)}) async-start(), calls=%async_computation.1 | async-start | bytes 1310720 | tf_op jit(solution)/shard_map/all_gather | solution.py:372
  32.1 26.6 %collective-permute-start.7 = (bf16[256,640]{1,0:T(8,128)(2,1)S(1)}, bf16[256,640]{1,0:T(8,128)(2,1)S(1)}, u32[]{:S(2)}, u32[]{:S(2)}) collective-permute-start(bf16[256,640]{1,0:T(8,128)(2,1)S(1)} %get-tuple-element.98.panel0.source), channel_id=1, source_target_pairs={{0,12},{1,13},{2,14},{3,15},{4,0},{5,1},{6,2},{7,3},{8,4},{9,5},{1... | collective-permute-start | bytes 983048 | tf_op jit(solution)/shard_map/ppermute | solution.py:363
  34.9 23.9 %collective-permute-start.8 = (bf16[256,640]{1,0:T(8,128)(2,1)S(1)}, bf16[256,640]{1,0:T(8,128)(2,1)S(1)}, u32[]{:S(2)}, u32[]{:S(2)}) collective-permute-start(bf16[256,640]{1,0:T(8,128)(2,1)S(1)} %get-tuple-element.98.panel0.source), channel_id=1, source_target_pairs={{0,8},{1,9},{2,10},{3,11},{4,12},{5,13},{6,14},{7,15},{8,0},{9,1},... | collective-permute-start | bytes 983048 | tf_op jit(solution)/shard_map/ppermute | solution.py:363
  35.2 23.5 %collective-permute-start.9 = (bf16[256,640]{1,0:T(8,128)(2,1)S(1)}, bf16[256,640]{1,0:T(8,128)(2,1)S(1)}, u32[]{:S(2)}, u32[]{:S(2)}) collective-permute-start(bf16[256,640]{1,0:T(8,128)(2,1)S(1)} %get-tuple-element.98.panel0.source), channel_id=1, source_target_pairs={{0,4},{1,5},{2,6},{3,7},{4,8},{5,9},{6,10},{7,11},{8,12},{9,13},{1... | collective-permute-start | bytes 983048 | tf_op jit(solution)/shard_map/ppermute | solution.py:363
  35.9 19.3 %collective-permute-start.10 = (bf16[2,64,256]{2,1,0:T(8,128)(2,1)S(1)}, bf16[2,64,256]{2,1,0:T(8,128)(2,1)S(1)}, u32[]{:S(2)}, u32[]{:S(2)}) collective-permute-start(bf16[2,64,256]{2,1,0:T(8,128)(2,1)S(1)} %copy-done.19), channel_id=1, source_target_pairs={{0,4},{1,5},{2,6},{3,7},{4,8},{5,9},{6,10},{7,11},{8,12},{9,13},{1... | collective-permute-start | bytes 196616 | tf_op jit(solution)/shard_map/ppermute | solution.py:363
  37.5 17.7 %collective-permute-start.11 = (bf16[2,64,256]{2,1,0:T(8,128)(2,1)S(1)}, bf16[2,64,256]{2,1,0:T(8,128)(2,1)S(1)}, u32[]{:S(2)}, u32[]{:S(2)}) collective-permute-start(bf16[2,64,256]{2,1,0:T(8,128)(2,1)S(1)} %copy-done.18), channel_id=1, source_target_pairs={{0,8},{1,9},{2,10},{3,11},{4,12},{5,13},{6,14},{7,15},{8,0},{9,1},... | collective-permute-start | bytes 196616 | tf_op jit(solution)/shard_map/ppermute | solution.py:363
  60.1 133.2 %all-gather.11.cloned.1.call-start = ((), (), s32[]{:S(2)}) async-start(), calls=%async_computation.2 | async-start | bytes 2621440 | tf_op jit(solution)/shard_map/all_gather | solution.py:372
  60.1 10.7 %collective-permute-start.4 = (bf16[2,64,1024]{2,1,0:T(8,128)(2,1)S(1)}, bf16[2,64,1024]{2,1,0:T(8,128)(2,1)S(1)}, u32[]{:S(2)}, u32[]{:S(2)}) collective-permute-start(bf16[2,64,1024]{2,1,0:T(8,128)(2,1)S(1)} %slice_bitcast_fusion.g0), channel_id=1, source_target_pairs={{0,1},{1,2},{2,3},{3,0},{4,5},{5,6},{6,7},{7,4},{8,9},{9,10},{10,1... | collective-permute-start | bytes 786440 | tf_op jit(solution)/shard_map/ppermute | solution.py:358
  60.8 16.0 %collective-permute-start.5 = (bf16[2,64,1024]{2,1,0:T(8,128)(2,1)S(1)}, bf16[2,64,1024]{2,1,0:T(8,128)(2,1)S(1)}, u32[]{:S(2)}, u32[]{:S(2)}) collective-permute-start(bf16[2,64,1024]{2,1,0:T(8,128)(2,1)S(1)} %slice_bitcast_fusion.g0), channel_id=1, source_target_pairs={{0,2},{1,3},{2,0},{3,1},{4,6},{5,7},{6,4},{7,5},{8,10},{9,11},{10,... | collective-permute-start | bytes 786440 | tf_op jit(solution)/shard_map/ppermute | solution.py:358
  63.7 13.1 %collective-permute-start.6 = (bf16[2,64,1024]{2,1,0:T(8,128)(2,1)S(1)}, bf16[2,64,1024]{2,1,0:T(8,128)(2,1)S(1)}, u32[]{:S(2)}, u32[]{:S(2)}) collective-permute-start(bf16[2,64,1024]{2,1,0:T(8,128)(2,1)S(1)} %slice_bitcast_fusion.g0), channel_id=1, source_target_pairs={{0,3},{1,0},{2,1},{3,2},{4,7},{5,4},{6,5},{7,6},{8,11},{9,8},{10,9... | collective-permute-start | bytes 786440 | tf_op jit(solution)/shard_map/ppermute | solution.py:358
  78.5 9.0 %collective-permute-start.13 = (bf16[256,640]{1,0:T(8,128)(2,1)S(1)}, bf16[256,640]{1,0:T(8,128)(2,1)S(1)}, u32[]{:S(2)}, u32[]{:S(2)}) collective-permute-start(bf16[256,640]{1,0:T(8,128)(2,1)S(1)} %get-tuple-element.102.panel0), channel_id=1, source_target_pairs={{0,12},{1,13},{2,14},{3,15},{4,0},{5,1},{6,2},{7,3},{8,4},{9,5},{1... | collective-permute-start | bytes 983048 | tf_op jit(solution)/shard_map/ppermute | solution.py:363
  80.9 9.4 %collective-permute-start.14 = (bf16[256,640]{1,0:T(8,128)(2,1)S(1)}, bf16[256,640]{1,0:T(8,128)(2,1)S(1)}, u32[]{:S(2)}, u32[]{:S(2)}) collective-permute-start(bf16[256,640]{1,0:T(8,128)(2,1)S(1)} %get-tuple-element.102.panel0), channel_id=1, source_target_pairs={{0,8},{1,9},{2,10},{3,11},{4,12},{5,13},{6,14},{7,15},{8,0},{9,1},... | collective-permute-start | bytes 983048 | tf_op jit(solution)/shard_map/ppermute | solution.py:363
  81.5 19.4 %collective-permute-start.15 = (bf16[256,640]{1,0:T(8,128)(2,1)S(1)}, bf16[256,640]{1,0:T(8,128)(2,1)S(1)}, u32[]{:S(2)}, u32[]{:S(2)}) collective-permute-start(bf16[256,640]{1,0:T(8,128)(2,1)S(1)} %get-tuple-element.102.panel0), channel_id=1, source_target_pairs={{0,4},{1,5},{2,6},{3,7},{4,8},{5,9},{6,10},{7,11},{8,12},{9,13},{1... | collective-permute-start | bytes 983048 | tf_op jit(solution)/shard_map/ppermute | solution.py:363
  82.2 31.5 %collective-permute-start.17 = (bf16[256,512]{1,0:T(8,128)(2,1)S(1)}, bf16[256,512]{1,0:T(8,128)(2,1)S(1)}, u32[]{:S(2)}, u32[]{:S(2)}) collective-permute-start(bf16[256,512]{1,0:T(8,128)(2,1)S(1)} %get-tuple-element.107.panel0), channel_id=1, source_target_pairs={{0,12},{1,13},{2,14},{3,15},{4,0},{5,1},{6,2},{7,3},{8,4},{9,5},{1... | collective-permute-start | bytes 786440 | tf_op jit(solution)/shard_map/ppermute | solution.py:363
  84.2 29.5 %collective-permute-start.18 = (bf16[256,512]{1,0:T(8,128)(2,1)S(1)}, bf16[256,512]{1,0:T(8,128)(2,1)S(1)}, u32[]{:S(2)}, u32[]{:S(2)}) collective-permute-start(bf16[256,512]{1,0:T(8,128)(2,1)S(1)} %get-tuple-element.107.panel0), channel_id=1, source_target_pairs={{0,8},{1,9},{2,10},{3,11},{4,12},{5,13},{6,14},{7,15},{8,0},{9,1},... | collective-permute-start | bytes 786440 | tf_op jit(solution)/shard_map/ppermute | solution.py:363
  88.2 25.4 %collective-permute-start.19 = (bf16[256,512]{1,0:T(8,128)(2,1)S(1)}, bf16[256,512]{1,0:T(8,128)(2,1)S(1)}, u32[]{:S(2)}, u32[]{:S(2)}) collective-permute-start(bf16[256,512]{1,0:T(8,128)(2,1)S(1)} %get-tuple-element.107.panel0), channel_id=1, source_target_pairs={{0,4},{1,5},{2,6},{3,7},{4,8},{5,9},{6,10},{7,11},{8,12},{9,13},{1... | collective-permute-start | bytes 786440 | tf_op jit(solution)/shard_map/ppermute | solution.py:363
  108.6 21.0 %collective-permute-start.16 = (bf16[256,640]{1,0:T(8,128)(2,1)S(1)}, bf16[256,640]{1,0:T(8,128)(2,1)S(1)}, u32[]{:S(2)}, u32[]{:S(2)}) collective-permute-start(bf16[256,640]{1,0:T(8,128)(2,1)S(1)} %get-tuple-element.105), channel_id=1, source_target_pairs={{0,16},{16,32},{32,48},{48,64},{64,80},{80,96},{96,112},{112,128},... | collective-permute-start | bytes 983048 | tf_op jit(solution)/shard_map/ppermute | solution.py:378
  115.8 9.6 %collective-permute-start.21 = (bf16[256,512]{1,0:T(8,128)(2,1)S(1)}, bf16[256,512]{1,0:T(8,128)(2,1)S(1)}, u32[]{:S(2)}, u32[]{:S(2)}) collective-permute-start(bf16[256,512]{1,0:T(8,128)(2,1)S(1)} %shard_map.105.panel0), channel_id=1, source_target_pairs={{0,8},{1,9},{2,10},{3,11},{4,12},{5,13},{6,14},{7,15},{8,0},{9,1},... | collective-permute-start | bytes 786440 | tf_op jit(solution)/shard_map/ppermute | solution.py:363
  117.4 12.2 %collective-permute-start.22 = (bf16[256,512]{1,0:T(8,128)(2,1)S(1)}, bf16[256,512]{1,0:T(8,128)(2,1)S(1)}, u32[]{:S(2)}, u32[]{:S(2)}) collective-permute-start(bf16[256,512]{1,0:T(8,128)(2,1)S(1)} %shard_map.105.panel0), channel_id=1, source_target_pairs={{0,4},{1,5},{2,6},{3,7},{4,8},{5,9},{6,10},{7,11},{8,12},{9,13},{1... | collective-permute-start | bytes 786440 | tf_op jit(solution)/shard_map/ppermute | solution.py:363
  133.8 8.8 %collective-permute-start.27 = (bf16[512,128]{1,0:T(8,128)(2,1)S(1)}, bf16[512,128]{1,0:T(8,128)(2,1)S(1)}, u32[]{:S(2)}, u32[]{:S(2)}) collective-permute-start(bf16[512,128]{1,0:T(8,128)(2,1)S(1)} %get-tuple-element.123), channel_id=1, source_target_pairs={{0,12},{1,13},{2,14},{3,15},{4,0},{5,1},{6,2},{7,3},{8,4},{9,5},{1... | collective-permute-start | bytes 393224 | tf_op jit(solution)/shard_map/ppermute | solution.py:363
  134.0 10.0 %collective-permute-start.28 = (bf16[512,128]{1,0:T(8,128)(2,1)S(1)}, bf16[512,128]{1,0:T(8,128)(2,1)S(1)}, u32[]{:S(2)}, u32[]{:S(2)}) collective-permute-start(bf16[512,128]{1,0:T(8,128)(2,1)S(1)} %get-tuple-element.123), channel_id=1, source_target_pairs={{0,8},{1,9},{2,10},{3,11},{4,12},{5,13},{6,14},{7,15},{8,0},{9,1},... | collective-permute-start | bytes 393224 | tf_op jit(solution)/shard_map/ppermute | solution.py:363
  135.3 14.0 %collective-permute-start.23 = (bf16[256,512]{1,0:T(8,128)(2,1)S(1)}, bf16[256,512]{1,0:T(8,128)(2,1)S(1)}, u32[]{:S(2)}, u32[]{:S(2)}) collective-permute-start(bf16[256,512]{1,0:T(8,128)(2,1)S(1)} %get-tuple-element.114), channel_id=1, source_target_pairs={{0,16},{16,32},{32,48},{48,64},{64,80},{80,96},{96,112},{112,128},... | collective-permute-start | bytes 786440 | tf_op jit(solution)/shard_map/ppermute | solution.py:378
  140.6 12.6 %collective-permute-start.24 = (bf16[256,512]{1,0:T(8,128)(2,1)S(1)}, bf16[256,512]{1,0:T(8,128)(2,1)S(1)}, u32[]{:S(2)}, u32[]{:S(2)}) collective-permute-start(bf16[256,512]{1,0:T(8,128)(2,1)S(1)} %get-tuple-element.124.block0.refs_0_.refs_1_), channel_id=1, source_target_pairs={{0,1},{1,2},{2,3},{3,0},{4,5},{5,6},{6,7},{7,4},{8,9},{9,10},{10,1... | collective-permute-start | bytes 786440 | tf_op jit(solution)/shard_map/ppermute | solution.py:358
  140.7 12.6 %collective-permute-start.25 = (bf16[256,512]{1,0:T(8,128)(2,1)S(1)}, bf16[256,512]{1,0:T(8,128)(2,1)S(1)}, u32[]{:S(2)}, u32[]{:S(2)}) collective-permute-start(bf16[256,512]{1,0:T(8,128)(2,1)S(1)} %get-tuple-element.124.block0.refs_0_.refs_1_), channel_id=1, source_target_pairs={{0,2},{1,3},{2,0},{3,1},{4,6},{5,7},{6,4},{7,5},{8,10},{9,11},{10,... | collective-permute-start | bytes 786440 | tf_op jit(solution)/shard_map/ppermute | solution.py:358
  142.6 11.6 %collective-permute-start.26 = (bf16[256,512]{1,0:T(8,128)(2,1)S(1)}, bf16[256,512]{1,0:T(8,128)(2,1)S(1)}, u32[]{:S(2)}, u32[]{:S(2)}) collective-permute-start(bf16[256,512]{1,0:T(8,128)(2,1)S(1)} %get-tuple-element.124.block0.refs_0_.refs_1_), channel_id=1, source_target_pairs={{0,3},{1,0},{2,1},{3,2},{4,7},{5,4},{6,5},{7,6},{8,11},{9,8},{10,9... | collective-permute-start | bytes 786440 | tf_op jit(solution)/shard_map/ppermute | solution.py:358
  157.4 8.9 %collective-permute-start.30 = (bf16[512,128]{1,0:T(8,128)(2,1)S(1)}, bf16[512,128]{1,0:T(8,128)(2,1)S(1)}, u32[]{:S(2)}, u32[]{:S(2)}) collective-permute-start(bf16[512,128]{1,0:T(8,128)(2,1)S(1)} %get-tuple-element.138), channel_id=1, source_target_pairs={{0,12},{1,13},{2,14},{3,15},{4,0},{5,1},{6,2},{7,3},{8,4},{9,5},{1... | collective-permute-start | bytes 393224 | tf_op jit(solution)/shard_map/ppermute | solution.py:363
  160.3 9.2 %collective-permute-start.32 = (bf16[512,128]{1,0:T(8,128)(2,1)S(1)}, bf16[512,128]{1,0:T(8,128)(2,1)S(1)}, u32[]{:S(2)}, u32[]{:S(2)}) collective-permute-start(bf16[512,128]{1,0:T(8,128)(2,1)S(1)} %get-tuple-element.138), channel_id=1, source_target_pairs={{0,4},{1,5},{2,6},{3,7},{4,8},{5,9},{6,10},{7,11},{8,12},{9,13},{1... | collective-permute-start | bytes 393224 | tf_op jit(solution)/shard_map/ppermute | solution.py:363
  172.1 9.7 %collective-permute-start.35 = (bf16[512,128]{1,0:T(8,128)(2,1)S(1)}, bf16[512,128]{1,0:T(8,128)(2,1)S(1)}, u32[]{:S(2)}, u32[]{:S(2)}) collective-permute-start(bf16[512,128]{1,0:T(8,128)(2,1)S(1)} %get-tuple-element.141), channel_id=1, source_target_pairs={{0,4},{1,5},{2,6},{3,7},{4,8},{5,9},{6,10},{7,11},{8,12},{9,13},{1... | collective-permute-start | bytes 393224 | tf_op jit(solution)/shard_map/ppermute | solution.py:363
  (32 other events, 323.4 us)
Sparse Core Ops, SparseCore 0:
  30.9 35.9 all-gather.6
  69.2 30.8 all-gather.8
  155.7 33.4 all-gather.10
